TPU v7x, 128 devices: a whole 4x4x4 slice. The times are simulated.
128 devices in a mesh: dp: 2 (over core), seq: 32 (over z, y, x_hi), fsdp: 2 (over x_lo).
Axes of the slice: x: 4 (x_hi: 2, x_lo: 2; x = x_hi * 2 + x_lo), y: 4, z: 4, core: 2. Of those that a mesh axis runs over, the one named last changes fastest.
Arguments:
- activations: bfloat16 [4, 8192, 1536], P(('dp', 'fsdp'), 'seq')
- cotangent: bfloat16 [4, 8192, 1536], P(('dp', 'fsdp'), 'seq'), may hold values from -6 to 6
- lengths: int32 [4], P(('dp', 'fsdp')), may hold values from 2048 to 8192, as said below
- poison: int32 [4, 32], P(('dp', 'fsdp'), 'seq'), may hold values from -1 to 255, as said below
- w_in: bfloat16 [1536, 3072], P('fsdp'), may hold values from -0.15625 to 0.15625
- taps: bfloat16 [1536, 32], P('fsdp'), may hold values from -1.5 to 1.5
Outputs:
- grad_input: bfloat16 [4, 8192, 1536], P(('dp', 'fsdp'), 'seq')
- update_in: float32 [1536, 3072], P(('dp', 'seq', 'fsdp'))
- update_taps: float32 [1536, 32], P(('dp', 'seq', 'fsdp'))
Inputs may be any that keep to these rules, and one draw needn't show every extreme that they name: `lengths`: utterance 0 has all 8192 frames valid. `poison`: each utterance has at most one entry other than -1; utterance 0 has none, and utterance 3 has one, at the last frame of its block.
All inputs are finite; a program needn't handle non-finite values.
Results may differ from a plain program's by a relative error of at most 0.01.
Values may be sent and summed in bfloat16 or wider, within the bound.
A program may use at most 128 MiB of HBM per device.

v0:
```python
import jax
import jax.numpy as jnp
from jax import lax
from jax.sharding import PartitionSpec as P


def extended(block, sides, width):
    for axis, dim in sides:
        count = lax.axis_size(axis)
        forward = [(i, i + 1) for i in range(count - 1)]
        backward = [(target, source) for source, target in forward]
        low = lax.ppermute(
            lax.slice_in_dim(block, block.shape[dim] - width, None, axis=dim), axis, forward
        )
        high = lax.ppermute(lax.slice_in_dim(block, 0, width, axis=dim), axis, backward)
        block = jnp.concatenate([low, block, high], axis=dim)
    return block


def normalize_rows(xf):
    row_average = jnp.mean(xf, axis=-1, keepdims=True)
    cent = xf - row_average
    var = jnp.mean(cent * cent, axis=-1, keepdims=True)
    inverse_deviation = lax.rsqrt(var + 1e-05)
    return (cent * inverse_deviation, inverse_deviation)


def body(activations, cotangent, lengths, poison, w_in, taps):
    rows = activations.shape[1]
    width = activations.shape[2]
    ntaps = taps.shape[1]
    half = ntaps // 2
    input_rows = activations[0]
    dy_rows = cotangent[0]
    local = lax.iota(jnp.int32, rows)
    frames = lax.axis_index("seq") * rows + local
    mask = (frames < lengths[0]).astype(jnp.float32)[:, None]
    centered_scaled, inverse_deviation = normalize_rows(input_rows.astype(jnp.float32))
    normalized_rows = centered_scaled.astype(jnp.bfloat16)
    w_piece = lax.all_gather(w_in, "fsdp", axis=0, tiled=True)
    t_piece = lax.all_gather(taps, "fsdp", axis=0, tiled=True)
    cols = normalized_rows
    acc = jnp.dot(cols, w_piece, preferred_element_type=jnp.float32)
    val = acc[:, :width]
    sig = jax.nn.sigmoid(acc[:, width:])
    glued = (val * sig * mask).astype(jnp.bfloat16)
    gpad = extended(glued, (("seq", 0),), half).astype(jnp.float32)
    tapsf = t_piece.astype(jnp.float32)
    conv = jnp.zeros((rows, width), jnp.float32)
    for k in range(ntaps):
        conv = conv + tapsf[:, k] * gpad[k : k + rows]
    swsig = jax.nn.sigmoid(conv)
    seen = jnp.where(
        local[:, None] == poison[0, 0], jnp.float32(jnp.inf), dy_rows.astype(jnp.float32)
    )
    row_bad = jnp.any(jnp.logical_not(jnp.isfinite(seen)), axis=1)
    all_frames = lax.axis_size("seq") * rows
    candidate = jnp.min(jnp.where(row_bad, frames, jnp.int32(all_frames)))
    first_bad = lax.pmin(candidate, "seq")
    cot = jnp.where((frames < first_bad)[:, None], dy_rows, jnp.zeros_like(dy_rows))
    dconv = (cot.astype(jnp.float32) * swsig * (1.0 + conv * (1.0 - swsig))).astype(jnp.bfloat16)
    dpad = extended(dconv, (("seq", 0),), half).astype(jnp.float32)
    dcf = dpad[half : half + rows]
    tap_terms = jnp.stack([jnp.sum(dcf * gpad[k : k + rows], axis=0) for k in range(ntaps)], axis=1)
    dglued = jnp.zeros((rows, width), jnp.float32)
    for k in range(ntaps):
        dglued = dglued + tapsf[:, k] * dpad[2 * half - k : 2 * half - k + rows]
    dglued = dglued * mask
    dpre = jnp.concatenate([dglued * sig, dglued * val * sig * (1.0 - sig)], axis=1).astype(
        jnp.bfloat16
    )
    grad_normalized = lax.dot_general(
        dpre,
        lax.all_gather(w_in, "fsdp", axis=0, tiled=True),
        (((1,), (1,)), ((), ())),
        preferred_element_type=jnp.float32,
    )
    inner_product = (
        grad_normalized
        - jnp.mean(grad_normalized, axis=-1, keepdims=True)
        - centered_scaled * jnp.mean(grad_normalized * centered_scaled, axis=-1, keepdims=True)
    )
    grad_rows = (inverse_deviation * inner_product).astype(jnp.bfloat16)
    cols = normalized_rows
    g_in = lax.psum_scatter(
        lax.dot_general(cols, dpre, (((0,), (0,)), ((), ())), preferred_element_type=jnp.float32),
        ("dp", "seq", "fsdp"),
        scatter_dimension=0,
        tiled=True,
    )
    g_taps = lax.psum_scatter(tap_terms, ("dp", "seq", "fsdp"), scatter_dimension=0, tiled=True)
    count_all = jnp.float32(2 * width * width + width * ntaps)
    local_sq = jnp.sum(g_in * g_in) + jnp.sum(g_taps * g_taps)
    total = lax.psum(local_sq, ("dp", "seq", "fsdp"))
    scale = 1.0 / jnp.maximum(jnp.float32(1.0), jnp.sqrt(total / count_all))
    return (grad_rows[None], g_in * scale, g_taps * scale)


def solution(mesh):
    placed = (
        P(("dp", "fsdp"), "seq", None),
        P(("dp", "fsdp"), "seq", None),
        P(("dp", "fsdp")),
        P(("dp", "fsdp"), "seq"),
        P("fsdp", None),
        P("fsdp", None),
    )
    return jax.shard_map(
        body,
        mesh=mesh,
        in_specs=placed,
        out_specs=(
            P(("dp", "fsdp"), "seq", None),
            P(("dp", "seq", "fsdp"), None),
            P(("dp", "seq", "fsdp"), None),
        ),
        check_vma=False,
    )
```

profile of v0, /device:TPU:1, one launch (start us, length us, event | category | flops | bytes accessed | tf_op | source)
XLA Modules:
  0.0 1038.6 jit_solution(5560634837687517773)
XLA Ops:
  9.8 19.3 %pmin.7 = s32[]{:T(128)} all-reduce(s32[]{:T(128)} %select_reduce_fusion), channel_id=1, replica_groups=mesh['dp'=2,'seq'=32,'fsdp'=2] {'seq'}, use_global_device_ids=true, to_apply=%region_4.5 | all-reduce | flops 1 | bytes 8 | tf_op jit(solution)/shard_map/pmin | solution.py:59
  29.8 4.7 all_gather.7
  36.0 98.5 %all-gather.2.cloned.1.call-done = bf16[1536,3072]{1,0:T(8,128)(2,1)} async-done(((bf16[768,3072]{1,0:T(8,128)(2,1)}), bf16[1536,3072]{1,0:T(8,128)(2,1)}) %all-gather.2.cloned.1.call-update) | async-done | bytes 9437200 | tf_op jit(solution)/shard_map/all_gather | solution.py:40
  134.5 5.4 fusion.56
  140.4 4.3 collective-permute-start
  146.7 4.4 collective-permute-done.1
  151.6 7.1 multiply_convert_fusion.2
  159.1 3.9 collective-permute-start.2
  164.3 5.0 collective-permute-done.3
  169.8 6.7 multiply_convert_fusion.1
  178.1 8.1 fusion.49
  186.2 408.9 %fusion = f32[16,3072]{1,0:T(8,128)} fusion(f32[1536,3072]{1,0:T(8,128)} %fusion.49), kind=kCustom, calls=%all-reduce-scatter | all-reduce-scatter fusion | flops 6291457 | bytes 19070976
  598.0 2.3 collective-permute-start.35
  619.7 2.1 collective-permute-start.25
  621.8 2.6 collective-permute-done.29
  626.3 2.9 multiply_reduce_fusion
  630.6 17.3 %collective-permute-start.23 = (f32[16,3072]{1,0:T(8,128)}, f32[16,3072]{1,0:T(8,128)S(1)}, u32[]{:S(2)}, u32[]{:S(2)}) collective-permute-start(f32[16,3072]{1,0:T(8,128)} %fusion), channel_id=1, source_target_pairs={{0,20},{1,21},{2,22},{3,23},{4,24},{5,25},{6,26},{7,27},{8,28},{9,... | collective-permute-start | bytes 589832
  647.9 5.2 collective-permute-start.22
  655.2 2.4 collective-permute-start.20
  663.4 17.0 %collective-permute-start.17 = (f32[16,3072]{1,0:T(8,128)}, f32[16,3072]{1,0:T(8,128)}, u32[]{:S(2)}, u32[]{:S(2)}) collective-permute-start(f32[16,3072]{1,0:T(8,128)} %fusion), channel_id=1, source_target_pairs={{0,14},{1,15},{2,16},{3,17},{4,18},{5,19},{6,20},{7,21},{8,22},{9,... | collective-permute-start | bytes 589832
  688.7 2.8 stack.131
  691.5 5.8 collective-permute-start.13
  697.3 3.4 collective-permute-start.12
  702.7 3.1 collective-permute-start.10
  705.8 2.8 collective-permute-start.9
  708.6 7.2 fusion.58
  715.8 6.2 collective-permute-done.13
  724.0 4.1 collective-permute-done.12
  733.9 33.1 %collective-permute-start.4 = (f32[16,3072]{1,0:T(8,128)}, f32[16,3072]{1,0:T(8,128)}, u32[]{:S(2)}, u32[]{:S(2)}) collective-permute-start(f32[16,3072]{1,0:T(8,128)} %fusion), channel_id=1, source_target_pairs={{0,1},{1,2},{2,3},{3,4},{4,5},{5,6},{6,7},{7,8},{8,9},{9,10},{10,1... | collective-permute-start | bytes 589832
  767.1 107.0 %all-reduce.5.cloned.1.call-done = f32[1536,32]{0,1:T(8,128)} async-done(((f32[1536,32]{0,1:T(8,128)}), f32[1536,32]{0,1:T(8,128)}) %all-reduce.5.cloned.1.call-update) | async-done | bytes 196624
  875.5 84.5 %concatenate.13 = f32[524,3072]{1,0:T(8,128)} concatenate(f32[12,3072]{1,0:T(8,128)S(1)} %copy-done.7, f32[16,3072]{1,0:T(8,128)} %collective-permute-done.34, f32[16,3072]{1,0:T(8,128)} %collective-permute-done.33, f32[16,3072]{1,0:T(8,128)} %collective-permute-done.32, f32[16,3072]{1,0:T(8,128)} %collective-permute-done.31, f32[16,3072]{1,0:T(8,128)} %collective-permute-done.30, ...), dimensions={0} | concatenate | bytes 12877824
  964.3 63.6 %psum.7 = f32[]{:T(128)} all-reduce(f32[]{:T(128)S(6)} %add.297), channel_id=1, replica_groups=mesh['dp'=2,'seq'=32,'fsdp'=2] {'dp','seq','fsdp'}, use_global_device_ids=true, to_apply=%region_43.44 | all-reduce | flops 1 | bytes 8 | tf_op jit(solution)/shard_map/psum | solution.py:94
  (298 shorter events, 67.1 us)
Async XLA Ops:
  7.2 127.3 %all-gather.2.cloned.1.call-start = ((), (), s32[]{:S(2)}) async-start(), calls=%async_computation | async-start | bytes 14155776 | tf_op jit(solution)/shard_map/all_gather | solution.py:40
  7.9 866.1 %all-reduce.5.cloned.1.call-start = ((), (), s32[]{:S(2)}) async-start(), calls=%async_computation.1 | async-start | bytes 393216
  595.1 15.2 %collective-permute-start.34 = (f32[16,3072]{1,0:T(8,128)}, f32[16,3072]{1,0:T(8,128)}, u32[]{:S(2)}, u32[]{:S(2)}) collective-permute-start(f32[16,3072]{1,0:T(8,128)} %fusion), channel_id=1, source_target_pairs={{0,31},{1,32},{2,33},{3,34},{4,35},{5,36},{6,37},{7,38},{8,39},{9,... | collective-permute-start | bytes 589832
  600.4 11.9 %collective-permute-start.33 = (f32[16,3072]{1,0:T(8,128)}, f32[16,3072]{1,0:T(8,128)}, u32[]{:S(2)}, u32[]{:S(2)}) collective-permute-start(f32[16,3072]{1,0:T(8,128)} %fusion), channel_id=1, source_target_pairs={{0,30},{1,31},{2,32},{3,33},{4,34},{5,35},{6,36},{7,37},{8,38},{9,... | collective-permute-start | bytes 589832
  602.3 13.5 %collective-permute-start.32 = (f32[16,3072]{1,0:T(8,128)}, f32[16,3072]{1,0:T(8,128)}, u32[]{:S(2)}, u32[]{:S(2)}) collective-permute-start(f32[16,3072]{1,0:T(8,128)} %fusion), channel_id=1, source_target_pairs={{0,29},{1,30},{2,31},{3,32},{4,33},{5,34},{6,35},{7,36},{8,37},{9,... | collective-permute-start | bytes 589832
  604.2 13.5 %collective-permute-start.31 = (f32[16,3072]{1,0:T(8,128)}, f32[16,3072]{1,0:T(8,128)}, u32[]{:S(2)}, u32[]{:S(2)}) collective-permute-start(f32[16,3072]{1,0:T(8,128)} %fusion), channel_id=1, source_target_pairs={{0,28},{1,29},{2,30},{3,31},{4,32},{5,33},{6,34},{7,35},{8,36},{9,... | collective-permute-start | bytes 589832
  610.3 14.1 %collective-permute-start.29 = (f32[16,3072]{1,0:T(8,128)}, f32[16,3072]{1,0:T(8,128)}, u32[]{:S(2)}, u32[]{:S(2)}) collective-permute-start(f32[16,3072]{1,0:T(8,128)} %fusion), channel_id=1, source_target_pairs={{0,26},{1,27},{2,28},{3,29},{4,30},{5,31},{6,32},{7,33},{8,34},{9,... | collective-permute-start | bytes 589832
  612.3 18.3 %collective-permute-start.28 = (f32[16,3072]{1,0:T(8,128)}, f32[16,3072]{1,0:T(8,128)S(1)}, u32[]{:S(2)}, u32[]{:S(2)}) collective-permute-start(f32[16,3072]{1,0:T(8,128)} %fusion), channel_id=1, source_target_pairs={{0,25},{1,26},{2,27},{3,28},{4,29},{5,30},{6,31},{7,32},{8,33},{9,... | collective-permute-start | bytes 589832
  615.8 32.1 %collective-permute-start.27 = (f32[16,3072]{1,0:T(8,128)}, f32[16,3072]{1,0:T(8,128)S(1)}, u32[]{:S(2)}, u32[]{:S(2)}) collective-permute-start(f32[16,3072]{1,0:T(8,128)} %fusion), channel_id=1, source_target_pairs={{0,24},{1,25},{2,26},{3,27},{4,28},{5,29},{6,30},{7,31},{8,32},{9,... | collective-permute-start | bytes 589832
  617.7 35.4 %collective-permute-start.26 = (f32[16,3072]{1,0:T(8,128)}, f32[16,3072]{1,0:T(8,128)S(1)}, u32[]{:S(2)}, u32[]{:S(2)}) collective-permute-start(f32[16,3072]{1,0:T(8,128)} %fusion), channel_id=1, source_target_pairs={{0,23},{1,24},{2,25},{3,26},{4,27},{5,28},{6,29},{7,30},{8,31},{9,... | collective-permute-start | bytes 589832
  619.7 35.5 %collective-permute-start.25 = (f32[16,3072]{1,0:T(8,128)}, f32[16,3072]{1,0:T(8,128)S(1)}, u32[]{:S(2)}, u32[]{:S(2)}) collective-permute-start(f32[16,3072]{1,0:T(8,128)} %fusion), channel_id=1, source_target_pairs={{0,22},{1,23},{2,24},{3,25},{4,26},{5,27},{6,28},{7,29},{8,30},{9,... | collective-permute-start | bytes 589832
  624.4 33.2 %collective-permute-start.24 = (f32[16,3072]{1,0:T(8,128)}, f32[16,3072]{1,0:T(8,128)S(1)}, u32[]{:S(2)}, u32[]{:S(2)}) collective-permute-start(f32[16,3072]{1,0:T(8,128)} %fusion), channel_id=1, source_target_pairs={{0,21},{1,22},{2,23},{3,24},{4,25},{5,26},{6,27},{7,28},{8,29},{9,... | collective-permute-start | bytes 589832
  630.6 30.9 %collective-permute-start.23 = (f32[16,3072]{1,0:T(8,128)}, f32[16,3072]{1,0:T(8,128)S(1)}, u32[]{:S(2)}, u32[]{:S(2)}) collective-permute-start(f32[16,3072]{1,0:T(8,128)} %fusion), channel_id=1, source_target_pairs={{0,20},{1,21},{2,22},{3,23},{4,24},{5,25},{6,26},{7,27},{8,28},{9,... | collective-permute-start | bytes 589832
  647.9 15.5 %collective-permute-start.22 = (f32[16,3072]{1,0:T(8,128)}, f32[16,3072]{1,0:T(8,128)S(1)}, u32[]{:S(2)}, u32[]{:S(2)}) collective-permute-start(f32[16,3072]{1,0:T(8,128)} %fusion), channel_id=1, source_target_pairs={{0,19},{1,20},{2,21},{3,22},{4,23},{5,24},{6,25},{7,26},{8,27},{9,... | collective-permute-start | bytes 589832
  653.2 27.3 %collective-permute-start.21 = (f32[16,3072]{1,0:T(8,128)}, f32[16,3072]{1,0:T(8,128)S(1)}, u32[]{:S(2)}, u32[]{:S(2)}) collective-permute-start(f32[16,3072]{1,0:T(8,128)} %fusion), channel_id=1, source_target_pairs={{0,18},{1,19},{2,20},{3,21},{4,22},{5,23},{6,24},{7,25},{8,26},{9,... | collective-permute-start | bytes 589832
  655.2 27.2 %collective-permute-start.20 = (f32[16,3072]{1,0:T(8,128)}, f32[16,3072]{1,0:T(8,128)S(1)}, u32[]{:S(2)}, u32[]{:S(2)}) collective-permute-start(f32[16,3072]{1,0:T(8,128)} %fusion), channel_id=1, source_target_pairs={{0,17},{1,18},{2,19},{3,20},{4,21},{5,22},{6,23},{7,24},{8,25},{9,... | collective-permute-start | bytes 589832
  657.6 26.7 %collective-permute-start.19 = (f32[16,3072]{1,0:T(8,128)}, f32[16,3072]{1,0:T(8,128)S(1)}, u32[]{:S(2)}, u32[]{:S(2)}) collective-permute-start(f32[16,3072]{1,0:T(8,128)} %fusion), channel_id=1, source_target_pairs={{0,16},{1,17},{2,18},{3,19},{4,20},{5,21},{6,22},{7,23},{8,24},{9,... | collective-permute-start | bytes 589832
  661.5 30.0 %collective-permute-start.18 = (f32[16,3072]{1,0:T(8,128)}, f32[16,3072]{1,0:T(8,128)}, u32[]{:S(2)}, u32[]{:S(2)}) collective-permute-start(f32[16,3072]{1,0:T(8,128)} %fusion), channel_id=1, source_target_pairs={{0,15},{1,16},{2,17},{3,18},{4,19},{5,20},{6,21},{7,22},{8,23},{9,... | collective-permute-start | bytes 589832
  663.4 33.9 %collective-permute-start.17 = (f32[16,3072]{1,0:T(8,128)}, f32[16,3072]{1,0:T(8,128)}, u32[]{:S(2)}, u32[]{:S(2)}) collective-permute-start(f32[16,3072]{1,0:T(8,128)} %fusion), channel_id=1, source_target_pairs={{0,14},{1,15},{2,16},{3,17},{4,18},{5,19},{6,20},{7,21},{8,22},{9,... | collective-permute-start | bytes 589832
  680.4 20.3 %collective-permute-start.16 = (f32[16,3072]{1,0:T(8,128)}, f32[16,3072]{1,0:T(8,128)}, u32[]{:S(2)}, u32[]{:S(2)}) collective-permute-start(f32[16,3072]{1,0:T(8,128)} %fusion), channel_id=1, source_target_pairs={{0,13},{1,14},{2,15},{3,16},{4,17},{5,18},{6,19},{7,20},{8,21},{9,... | collective-permute-start | bytes 589832
  682.4 20.3 %collective-permute-start.15 = (f32[16,3072]{1,0:T(8,128)}, f32[16,3072]{1,0:T(8,128)}, u32[]{:S(2)}, u32[]{:S(2)}) collective-permute-start(f32[16,3072]{1,0:T(8,128)} %fusion), channel_id=1, source_target_pairs={{0,12},{1,13},{2,14},{3,15},{4,16},{5,17},{6,18},{7,19},{8,20},{9,... | collective-permute-start | bytes 589832
  684.3 21.4 %collective-permute-start.14 = (f32[16,3072]{1,0:T(8,128)}, f32[16,3072]{1,0:T(8,128)}, u32[]{:S(2)}, u32[]{:S(2)}) collective-permute-start(f32[16,3072]{1,0:T(8,128)} %fusion), channel_id=1, source_target_pairs={{0,11},{1,12},{2,13},{3,14},{4,15},{5,16},{6,17},{7,18},{8,19},{9,... | collective-permute-start | bytes 589832
  691.5 30.5 %collective-permute-start.13 = (f32[16,3072]{1,0:T(8,128)}, f32[16,3072]{1,0:T(8,128)}, u32[]{:S(2)}, u32[]{:S(2)}) collective-permute-start(f32[16,3072]{1,0:T(8,128)} %fusion), channel_id=1, source_target_pairs={{0,10},{1,11},{2,12},{3,13},{4,14},{5,15},{6,16},{7,17},{8,18},{9,... | collective-permute-start | bytes 589832
  697.3 30.8 %collective-permute-start.12 = (f32[16,3072]{1,0:T(8,128)}, f32[16,3072]{1,0:T(8,128)}, u32[]{:S(2)}, u32[]{:S(2)}) collective-permute-start(f32[16,3072]{1,0:T(8,128)} %fusion), channel_id=1, source_target_pairs={{0,9},{1,10},{2,11},{3,12},{4,13},{5,14},{6,15},{7,16},{8,17},{9,1... | collective-permute-start | bytes 589832
  700.8 29.3 %collective-permute-start.11 = (f32[16,3072]{1,0:T(8,128)}, f32[16,3072]{1,0:T(8,128)}, u32[]{:S(2)}, u32[]{:S(2)}) collective-permute-start(f32[16,3072]{1,0:T(8,128)} %fusion), channel_id=1, source_target_pairs={{0,8},{1,9},{2,10},{3,11},{4,12},{5,13},{6,14},{7,15},{8,16},{9,17... | collective-permute-start | bytes 589832
  702.7 29.3 %collective-permute-start.10 = (f32[16,3072]{1,0:T(8,128)}, f32[16,3072]{1,0:T(8,128)}, u32[]{:S(2)}, u32[]{:S(2)}) collective-permute-start(f32[16,3072]{1,0:T(8,128)} %fusion), channel_id=1, source_target_pairs={{0,7},{1,8},{2,9},{3,10},{4,11},{5,12},{6,13},{7,14},{8,15},{9,16}... | collective-permute-start | bytes 589832
  705.8 28.1 %collective-permute-start.9 = (f32[16,3072]{1,0:T(8,128)}, f32[16,3072]{1,0:T(8,128)}, u32[]{:S(2)}, u32[]{:S(2)}) collective-permute-start(f32[16,3072]{1,0:T(8,128)} %fusion), channel_id=1, source_target_pairs={{0,6},{1,7},{2,8},{3,9},{4,10},{5,11},{6,12},{7,13},{8,14},{9,15},... | collective-permute-start | bytes 589832
  722.1 153.4 %collective-permute-start.8 = (f32[16,3072]{1,0:T(8,128)}, f32[16,3072]{1,0:T(8,128)}, u32[]{:S(2)}, u32[]{:S(2)}) collective-permute-start(f32[16,3072]{1,0:T(8,128)} %fusion), channel_id=1, source_target_pairs={{0,5},{1,6},{2,7},{3,8},{4,9},{5,10},{6,11},{7,12},{8,13},{9,14},{... | collective-permute-start | bytes 589832
  728.1 147.3 %collective-permute-start.7 = (f32[16,3072]{1,0:T(8,128)}, f32[16,3072]{1,0:T(8,128)}, u32[]{:S(2)}, u32[]{:S(2)}) collective-permute-start(f32[16,3072]{1,0:T(8,128)} %fusion), channel_id=1, source_target_pairs={{0,4},{1,5},{2,6},{3,7},{4,8},{5,9},{6,10},{7,11},{8,12},{9,13},{1... | collective-permute-start | bytes 589832
  730.0 145.4 %collective-permute-start.6 = (f32[16,3072]{1,0:T(8,128)}, f32[16,3072]{1,0:T(8,128)}, u32[]{:S(2)}, u32[]{:S(2)}) collective-permute-start(f32[16,3072]{1,0:T(8,128)} %fusion), channel_id=1, source_target_pairs={{0,3},{1,4},{2,5},{3,6},{4,7},{5,8},{6,9},{7,10},{8,11},{9,12},{10... | collective-permute-start | bytes 589832
  732.0 143.5 %collective-permute-start.5 = (f32[16,3072]{1,0:T(8,128)}, f32[16,3072]{1,0:T(8,128)}, u32[]{:S(2)}, u32[]{:S(2)}) collective-permute-start(f32[16,3072]{1,0:T(8,128)} %fusion), channel_id=1, source_target_pairs={{0,2},{1,3},{2,4},{3,5},{4,6},{5,7},{6,8},{7,9},{8,10},{9,11},{10,... | collective-permute-start | bytes 589832
  733.9 141.6 %collective-permute-start.4 = (f32[16,3072]{1,0:T(8,128)}, f32[16,3072]{1,0:T(8,128)}, u32[]{:S(2)}, u32[]{:S(2)}) collective-permute-start(f32[16,3072]{1,0:T(8,128)} %fusion), channel_id=1, source_target_pairs={{0,1},{1,2},{2,3},{3,4},{4,5},{5,6},{6,7},{7,8},{8,9},{9,10},{10,1... | collective-permute-start | bytes 589832
  (96 other events, 5565.3 us)
Sparse Core Ops, SparseCore 0:
  9.7 124.7 all-gather.1
  691.6 182.4 all-reduce.4
where the time goes:
time: 1040 us
  blocking collectives  497 us (48%)
  waiting for transfers between devices  233 us (22%)
  starting transfers between devices  146 us (14%)
  local copies, waits for them, and re-layouts  91.5 us (9%)
  other arithmetic  31.1 us (3%)
  matrix products  20.7 us (2%)
  between operations  19.7 us (2%)
    unnamed x1, blocking collectives  409 us
    unnamed x33, starting transfers between devices  135 us
    unnamed x35, waiting for transfers between devices  125 us
    all_gather x1, waiting for transfers between devices, body(): w_piece = lax.all_gather(w_in, 'fsdp', axis=0, tiled=True)  98.5 us
    unnamed x183, local copies, waits for them, and re-layouts  88 us
    psum x1, blocking collectives, body(): total = lax.psum(local_sq, ('dp', 'seq', 'fsdp'))  63.6 us
  transfers between devices with their start and end apart: 38, of which 10 were waited for; matrix products, arithmetic and copies ran while one was open for 2% of the time, Pallas kernels for 0%

commit v1 on v0

v1 whole, which is shorter than its diff:
```python
import functools

import jax
import jax.numpy as jnp
from jax import lax
from jax.experimental import pallas as pl
from jax.experimental.pallas import tpu as pltpu
from jax.sharding import PartitionSpec as P

MESH = pl.DeviceIdType.MESH
F32 = jnp.float32
BF16 = jnp.bfloat16

D = 1536
H = 768
KT = 32
ROWS = 256
FRAMES = 8192
NC = 6
CH = 128
BIG = FRAMES


def sigmoid(v):
    return 0.5 * jnp.tanh(0.5 * v) + 0.5


def dot(a, b, dims=(((1,), (0,)), ((), ()))):
    return lax.dot_general(a, b, dims, preferred_element_type=F32)


def iota(shape, dim):
    return lax.broadcasted_iota(jnp.int32, shape, dim)


def one_hot(flag):
    return jnp.where(flag, jnp.float32(1.0), jnp.float32(0.0)).astype(BF16)


def await_bytes(ref, sem):
    pltpu.make_async_copy(ref, ref, sem).wait()


def kernel(
    len_ref, poi_ref, taps_ref, x_hbm, cot_hbm, w_hbm,
    gx_ref, gin_ref, gtap_ref,
    x_vm, cot_vm, cot_sib, cot_halo, nn, halo, na, nt, w_vm, cp, cph,
    tap_in, tapf, tb, msk, stat, pre, val_s, sig_s, xe, xh, de, dh, dp, dpn,
    tg, tt, g, r1, s1, r2, fs, r3, sf, t_r1, t_s1, t_r2,
    dno, dns, dnr, fb_s, fb_r, ps_s, ps_r,
    local_sem, w_loc, w_send, w_recv, misc_send, misc_recv, fb_send, fb_recv,
    r1_send, r1_recv, r2_send, r2_recv, r3_send, r3_recv, t_send, t_recv, ps_send, ps_recv,
):
    c = lax.axis_index("dp")
    s = lax.axis_index("seq")
    f = lax.axis_index("fsdp")
    z, y = s // 8, (s // 2) % 4
    x = (s % 2) * 2 + f
    oc = 1 - c

    def dev(core, zz, yy, xx):
        return (core, zz * 8 + yy * 2 + xx // 2, xx % 2)

    def xd(d):
        return (x + d) % 4

    def yd(d):
        return (y + d) % 4

    def zd(d):
        return (z + d) % 4

    nxt, prv = (s + 1) % 32, (s + 31) % 32
    sibling = dev(oc, z, y, x)

    def send(src, dst, send_sem, recv_sem, device):
        pltpu.make_async_remote_copy(
            src_ref=src, dst_ref=dst, send_sem=send_sem, recv_sem=recv_sem,
            device_id=device, device_id_type=MESH,
        ).start()

    partners = [sibling]
    partners += [dev(e, z, y, xd(d)) for d in (1, 2, 3) for e in (0, 1)]
    partners += [dev(c, z, yd(d), x) for d in (1, 2, 3)]
    partners += [dev(c, zd(d), y, x) for d in (1, 2, 3)]
    partners += [(e, q, f) for q in (prv, nxt) for e in (0, 1)]
    barrier = pltpu.get_barrier_semaphore()
    for partner in partners:
        pl.semaphore_signal(barrier, inc=1, device_id=partner, device_id_type=MESH)

    load_x = pltpu.make_async_copy(x_hbm.at[0], x_vm, local_sem.at[0])
    load_cot = pltpu.make_async_copy(cot_hbm.at[0], cot_vm, local_sem.at[1])
    load_cot.start()
    load_x.start()

    def w_columns(j, part):
        return pl.ds(pl.multiple_of(part * D + c * H + j * CH, CH), CH)

    def local_w(j):
        for part in (0, 1):
            pltpu.make_async_copy(
                w_hbm.at[:, w_columns(j, part)],
                w_vm.at[j, pl.ds(pl.multiple_of(f * H, H), H), pl.ds(part * CH, CH)],
                w_loc.at[j],
            ).start()

    def send_w(j):
        for side in (0, 1):
            for part in (0, 1):
                send(
                    w_hbm.at[pl.ds(side * (H // 2), H // 2), w_columns(j, part)],
                    w_vm.at[
                        j,
                        pl.ds(pl.multiple_of(f * H + side * (H // 2), H // 2), H // 2),
                        pl.ds(part * CH, CH),
                    ],
                    w_send.at[j], w_recv.at[j, side], dev(c, z, y, xd(1 if side == 0 else 3)),
                )

    def await_w(j):
        await_bytes(w_vm.at[j, pl.ds(pl.multiple_of(f * H, H), H)], w_loc.at[j])
        for side in (0, 1):
            base = pl.multiple_of((1 - f) * H + side * (H // 2), H // 2)
            await_bytes(w_vm.at[j, pl.ds(base, H // 2)], w_recv.at[j, side])

    for j in range(2):
        local_w(j)

    frame0 = s * ROWS
    load_cot.wait()
    spoiled = jnp.zeros((ROWS, 128), F32)
    for i in range(D // 128):
        spoiled = spoiled + cot_vm[:, i * 128 : (i + 1) * 128].astype(F32) * 0.0
    local = iota((ROWS, 128), 0)
    bad = jnp.logical_or(spoiled != 0.0, local == poi_ref[0, 0])
    cand = jnp.where(bad, frame0 + local, jnp.int32(BIG))
    cand = jnp.min(cand.reshape(ROWS // 8, 8, 128), axis=0)
    cand = jnp.min(jnp.min(cand, axis=0, keepdims=True), axis=1, keepdims=True)
    row = iota((8, 128), 0)
    tile = jnp.where(row == c, jnp.broadcast_to(cand, (8, 128)), jnp.int32(BIG))
    fb_s[0] = jnp.where(row == 2 + c, len_ref[0], tile)

    pl.semaphore_wait(barrier, len(partners))

    send_w(0)
    for k, partner in enumerate((sibling, dev(c, z, y, xd(2)), dev(oc, z, y, xd(2)))):
        send(fb_s.at[0], fb_r.at[0, k], fb_send.at[0], fb_recv.at[0], partner)
    send(
        cot_vm.at[:, pl.ds(pl.multiple_of(oc * H, H), H)], cot_sib,
        misc_send.at[0], misc_recv.at[0], sibling,
    )
    for e in (0, 1):
        cols = pl.ds(e * H, H)
        send(cot_vm.at[pl.ds(ROWS - 16, 16), cols], cot_halo.at[c, 0],
             misc_send.at[1], misc_recv.at[1], (e, nxt, f))
        send(cot_vm.at[pl.ds(0, 16), cols], cot_halo.at[c, 1],
             misc_send.at[1], misc_recv.at[1], (e, prv, f))
    send(taps_ref, tap_in, misc_send.at[2], misc_recv.at[2], dev(c, z, y, xd(3)))
    send_w(1)

    load_x.wait()

    def norm_rows(i, _):
        rows = pl.ds(pl.multiple_of(i * 32, 32), 32)
        xf = x_vm[rows, :].astype(F32)
        average = jnp.mean(xf, axis=-1, keepdims=True)
        cent = xf - average
        inverse = lax.rsqrt(jnp.mean(cent * cent, axis=-1, keepdims=True) + 1e-05)
        nn[rows, :] = (cent * inverse).astype(BF16)
        stat[0, rows, :] = jnp.broadcast_to(average, (32, 128))
        stat[1, rows, :] = jnp.broadcast_to(inverse, (32, 128))
        return 0

    lax.fori_loop(0, ROWS // 32, norm_rows, 0)
    send(nn.at[pl.ds(ROWS - 32, 32)], halo.at[c, 0], misc_send.at[3], misc_recv.at[3], (c, nxt, f))
    send(nn.at[pl.ds(0, 32)], halo.at[c, 1], misc_send.at[3], misc_recv.at[3], (c, prv, f))

    r0, r1i = iota((ROWS, ROWS), 0), iota((ROWS, ROWS), 1)
    to_phase = one_hot((r0 % 8) * 32 + r0 // 8 == r1i)
    own_rows = pl.ds(pl.multiple_of(c * ROWS, ROWS), ROWS)
    sib_rows = pl.ds(pl.multiple_of(oc * ROWS, ROWS), ROWS)
    na[own_rows, :] = dot(to_phase, nn[...]).astype(BF16)
    send(na.at[own_rows], na.at[own_rows], misc_send.at[4], misc_recv.at[4], sibling)

    await_bytes(fb_r.at[0], fb_recv.at[0])
    fb_s[1] = jnp.minimum(jnp.minimum(fb_s[0], fb_r[0, 0]), jnp.minimum(fb_r[0, 1], fb_r[0, 2]))
    for d in (1, 2, 3):
        send(fb_s.at[1], fb_r.at[1, d - 1], fb_send.at[1], fb_recv.at[1], dev(c, z, yd(d), x))

    for i in range(D // 128):
        cols = pl.ds(i * 128, 128)
        nt[cols, own_rows] = na[own_rows, cols].T

    await_bytes(halo.at[c], misc_recv.at[3])
    send(halo.at[c], halo.at[c], misc_send.at[5], misc_recv.at[5], sibling)

    await_bytes(fb_r.at[1], fb_recv.at[1])
    fb_s[2] = jnp.minimum(jnp.minimum(fb_s[1], fb_r[1, 0]), jnp.minimum(fb_r[1, 1], fb_r[1, 2]))
    for d in (1, 2, 3):
        send(fb_s.at[2], fb_r.at[2, d - 1], fb_send.at[2], fb_recv.at[2], dev(c, zd(d), y, x))

    await_bytes(tap_in, misc_recv.at[2])
    mine = jnp.where(f == c, jnp.float32(1.0), jnp.float32(0.0))
    tapf[...] = taps_ref[...].astype(F32) * mine + tap_in[...].astype(F32) * (1.0 - mine)

    await_bytes(na.at[sib_rows], misc_recv.at[4])
    for i in range(D // 128):
        cols = pl.ds(i * 128, 128)
        nt[cols, sib_rows] = na[sib_rows, cols].T
    await_bytes(halo.at[oc], misc_recv.at[5])
    h0, h1 = iota((128, 128), 0), iota((128, 128), 1)
    source = ((h0 % 4) * 32) + ((h0 // 4) % 2) * 16 + h0 // 8
    halo_order = one_hot(source == h1)
    na[512:640, :] = dot(halo_order, halo[...].reshape(128, D)).astype(BF16)

    await_bytes(fb_r.at[2], fb_recv.at[2])
    votes = jnp.minimum(jnp.minimum(fb_s[2], fb_r[2, 0]), jnp.minimum(fb_r[2, 1], fb_r[2, 2]))
    await_bytes(cot_sib, misc_recv.at[0])
    await_bytes(cot_halo, misc_recv.at[1])
    ra = iota((ROWS, 128), 0)
    frame = frame0 + (ra % 8) * 32 + ra // 8
    for own in (True, False):
        if own:
            part = cot_vm[:, pl.ds(pl.multiple_of(c * H, H), H)]
            u = c
        else:
            part = cot_sib[...]
            u = oc
        first = jnp.min(
            jnp.where(iota((8, 128), 0) == u, votes, jnp.int32(BIG)), axis=0, keepdims=True
        )
        keep = jnp.where(frame < first, jnp.float32(1.0), jnp.float32(0.0))
        moved = dot(to_phase, part)
        for i in range(NC):
            cp[u, :, i * CH : (i + 1) * CH] = (moved[:, i * CH : (i + 1) * CH] * keep).astype(BF16)
    c0, c1 = iota((128, 64), 0), iota((128, 64), 1)
    edge_order = one_hot(
        jnp.logical_and(c0 % 8 < 4, (c0 % 8) * 16 + c0 // 8 == c1)
    )
    hr = iota((128, 128), 0)
    place, q = hr % 8, hr // 8
    edge_frame = frame0 + jnp.where(place % 2 == 0, q - 16, q + ROWS)
    limit = jnp.where((place // 2) % 2 == 0, votes[0:1], votes[1:2])
    keep = jnp.logical_and(edge_frame >= 0, edge_frame < limit)
    keep = jnp.where(keep, jnp.float32(1.0), jnp.float32(0.0))
    moved = dot(edge_order, cot_halo[...].reshape(64, H))
    for i in range(NC):
        cph[:, i * CH : (i + 1) * CH] = (moved[:, i * CH : (i + 1) * CH] * keep).astype(BF16)

    for u in (0, 1):
        msk[u * ROWS : (u + 1) * ROWS, :] = jnp.where(
            frame < votes[2 + u : 3 + u], jnp.float32(1.0), jnp.float32(0.0)
        )
    halo_frame = frame0 + jnp.where(place % 2 == 0, q - 32, q + ROWS) + (place // 4) * 16
    limit = jnp.where((place // 2) % 2 == 0, votes[2:3], votes[3:4])
    keep = jnp.logical_and(halo_frame >= 0, halo_frame < limit)
    msk[512:640, :] = jnp.where(keep, jnp.float32(1.0), jnp.float32(0.0))

    from_phase = one_hot((r1i % 8) * 32 + r1i // 8 == r0)

    def stage1_start(j):
        for d in (1, 2, 3):
            send(g.at[j, 0, :, zd(d)], r1.at[j, 0, d - 1], r1_send.at[j, 0], r1_recv.at[j, 0],
                 dev(c, zd(d), y, x))
            send(g.at[j, 1, :, :, yd(d)], r1.at[j, 1, d - 1], r1_send.at[j, 1], r1_recv.at[j, 1],
                 dev(c, z, yd(d), x))

    def stage1_finish(j):
        for part in (0, 1):
            await_bytes(r1.at[j, part], r1_recv.at[j, part])

            def add(i, _):
                a, b = i // 4, i % 4
                mine = g[j, 0, a, z, b] if part == 0 else g[j, 1, a, b, y]
                total = mine.astype(F32)
                for d in range(3):
                    total = total + r1[j, part, d, a, b].astype(F32)
                s1[j, part, a, b] = total.astype(BF16)
                return 0

            lax.fori_loop(0, 8, add, 0)
        for d in (1, 2, 3):
            send(s1.at[j, 0, :, yd(d)], r2.at[j, 0, d - 1], r2_send.at[j, 0], r2_recv.at[j, 0],
                 dev(c, z, yd(d), x))
            send(s1.at[j, 1, :, zd(d)], r2.at[j, 1, d - 1], r2_send.at[j, 1], r2_recv.at[j, 1],
                 dev(c, zd(d), y, x))

    def stage2_finish(j):
        for part in (0, 1):
            await_bytes(r2.at[j, part], r2_recv.at[j, part])
            lanes = pl.ds(pl.multiple_of(j * 256 + part * 128, 128), 128)
            for a in (0, 1):
                total = s1[j, part, a, y if part == 0 else z].astype(F32)
                for d in range(3):
                    total = total + r2[j, part, d, a].astype(F32)
                sf[a, 0:48] = total
                for b in range(4):
                    fs[a, b, :, lanes] = sf[a, 12 * b : 12 * b + 16].astype(BF16)

    sf[...] = jnp.zeros_like(sf)
    tg[...] = jnp.zeros_like(tg)
    for a in (0, 1):
        for b in range(4):
            fs[a, b, :, 1536:1664] = jnp.zeros((16, 128), BF16)

    sub = iota((16, 8, 128), 1)

    def chunk(j, _):
        @pl.when(j + 2 < NC)
        def _():
            local_w(j + 2)
            send_w(j + 2)

        lanes = pl.ds(pl.multiple_of(j * CH, CH), CH)
        for k in range(KT):
            tb[k] = jnp.broadcast_to(tapf[k : k + 1, lanes], (8, 128))
        await_w(j)
        pre[...] = dot(na[...], w_vm[j])

        def gated(rows):
            sig = sigmoid(pre[rows, CH:])
            val = pre[rows, :CH]
            return val, sig, val * sig * msk[rows, :]

        main = []
        for u in (0, 1):
            rows = slice(u * ROWS, (u + 1) * ROWS)
            val, sig, glued = gated(rows)
            val_s[rows, :] = val
            sig_s[rows, :] = sig
            xe[u, 16:48] = glued.reshape(32, 8, CH)
        h3 = gated(slice(512, 640))[2].reshape(16, 8, CH)
        h4 = pltpu.roll(h3, 4, 1)
        for u in (0, 1):
            left = h4 if u == 0 else pltpu.roll(h3, 2, 1)
            xe[u, 0:16] = jnp.where(sub == 0, left, pltpu.roll(xe[u, 32:48], 1, 1))
            xe[u, 48:64] = jnp.where(
                sub == 7, pltpu.roll(h3, 6 - 2 * u, 1), pltpu.roll(xe[u, 16:32], 7, 1)
            )
        xh[0:16] = jnp.where(
            sub == 1, pltpu.roll(xe[0, 32:48], 2, 1),
            jnp.where(sub == 3, pltpu.roll(xe[1, 32:48], 4, 1), h3),
        )
        xh[16:32] = jnp.where(sub % 2 == 0, h4, h3)
        xh[32:48] = jnp.where(
            sub == 0, xe[0, 16:32], jnp.where(sub == 2, pltpu.roll(xe[1, 16:32], 2, 1), h4)
        )

        def conv(window):
            total = tb[0][None] * window[0:8]
            for k in range(1, KT):
                total = total + tb[k][None] * window[k : k + 8]
            return total

        def through_swish(total, cot):
            gate = sigmoid(total)
            return cot * gate * (1.0 + total * (1.0 - gate))

        def forward(i, _):
            u, b = i // 4, i % 4
            total = conv(xe[u, pl.ds(b * 8, 39)])
            cot = cp[u, pl.ds(pl.multiple_of(b * 64, 64), 64), lanes].astype(F32)
            de[u, pl.ds(16 + b * 8, 8)] = through_swish(total, cot.reshape(8, 8, CH))
            return 0

        lax.fori_loop(0, 8, forward, 0)

        def forward_edge(b, _):
            total = conv(xh[pl.ds(b * 8, 39)])
            cot = cph[pl.ds(pl.multiple_of(b * 64, 64), 64), lanes].astype(F32)
            dh[pl.ds(b * 8, 8)] = through_swish(total, cot.reshape(8, 8, CH))
            return 0

        lax.fori_loop(0, 2, forward_edge, 0)
        d3 = dh[...]
        for u in (0, 1):
            left = d3 if u == 0 else pltpu.roll(d3, 6, 1)
            de[u, 0:16] = jnp.where(sub == 0, left, pltpu.roll(de[u, 32:48], 1, 1))
            de[u, 48:64] = jnp.where(
                sub == 7, pltpu.roll(d3, 6 - 2 * u, 1), pltpu.roll(de[u, 16:32], 7, 1)
            )

        def backward(i, _):
            u, b = i // 4, i % 4
            window = de[u, pl.ds(b * 8 + 1, 39)]
            total = tb[0][None] * window[31:39]
            for k in range(1, KT):
                total = total + tb[k][None] * window[31 - k : 39 - k]
            rows = pl.ds(pl.multiple_of(i * 64, 64), 64)
            dglued = total.reshape(64, CH) * msk[rows, :]
            val, sig = val_s[rows, :], sig_s[rows, :]
            dval = dglued * sig
            dp[rows, 0:CH] = dval.astype(BF16)
            dp[rows, CH:] = (dval * val * (1.0 - sig)).astype(BF16)
            return 0

        lax.fori_loop(0, 8, backward, 0)

        def tap_terms(i, total):
            u, b = i // 4, i % 4
            window = xe[u, pl.ds(b * 8, 39)]
            grads = de[u, pl.ds(16 + b * 8, 8)]
            for m in range(8):
                total = total + grads[m][None] * window[m : m + 32]
            return total

        terms = lax.fori_loop(0, 8, tap_terms, jnp.zeros((KT, 8, CH), F32))
        tg[j, 0:KT] = jnp.sum(terms, axis=1)

        for i in range(8):
            grad = dot(nt[i * 192 : (i + 1) * 192, :], dp[...])
            for part in (0, 1):
                half = grad[:, part * CH : (part + 1) * CH].astype(BF16)
                g[j, part, i // 4, i % 4] = half.reshape(4, 48, CH)
        stage1_start(j)
        for u in (0, 1):
            rows = slice(u * ROWS, (u + 1) * ROWS)
            dpn[j, rows, :] = dot(from_phase, dp[rows, :]).astype(BF16)

        @pl.when(j >= 1)
        def _():
            stage1_finish(j - 1)

        @pl.when(j >= 2)
        def _():
            stage2_finish(j - 2)

        return 0

    lax.fori_loop(0, NC, chunk, 0)

    for j in range(NC):
        tt[j * CH : (j + 1) * CH, :] = tg[j].T.astype(BF16)
    for d in (1, 2, 3):
        send(tt.at[pl.ds(pl.multiple_of(zd(d) * 192, 16), 192)], t_r1.at[d - 1],
             t_send.at[0], t_recv.at[0], dev(c, zd(d), y, x))

    dims = (((1,), (1,)), ((), ()))

    def dnormed(u, cols):
        rows = pl.ds(pl.multiple_of(u * ROWS, ROWS), ROWS)
        total = dot(dpn[0, rows, :], w_vm[0, cols, :], dims)
        for j in range(1, NC):
            total = total + dot(dpn[j, rows, :], w_vm[j, cols, :], dims)
        return total

    def sibling_part(i, _):
        cols = pl.ds(pl.multiple_of(i * 256, 256), 256)
        dns[:, cols] = dnormed(oc, cols).astype(BF16)
        return 0

    lax.fori_loop(0, D // 256, sibling_part, 0)
    send(dns, dnr, misc_send.at[6], misc_recv.at[6], sibling)

    stage1_finish(NC - 1)
    stage2_finish(NC - 2)
    await_bytes(t_r1, t_recv.at[0])
    mine = tt[pl.ds(pl.multiple_of(z * 192, 16), 192), :].astype(F32)
    for d in range(3):
        mine = mine + t_r1[d].astype(F32)
    t_s1[...] = mine.astype(BF16)
    for d in (1, 2, 3):
        send(t_s1.at[pl.ds(pl.multiple_of(yd(d) * 48, 16), 48)], t_r2.at[d - 1],
             t_send.at[1], t_recv.at[1], dev(c, z, yd(d), x))

    def own_part(i, _):
        cols = pl.ds(pl.multiple_of(i * 256, 256), 256)
        dno[:, cols] = dnormed(c, cols)
        return 0

    lax.fori_loop(0, D // 256, own_part, 0)

    stage2_finish(NC - 1)
    await_bytes(t_r2, t_recv.at[1])
    mine = t_s1[pl.ds(pl.multiple_of(y * 48, 16), 48), :].astype(F32)
    for d in range(3):
        mine = mine + t_r2[d].astype(F32)
    sf[0, 0:48] = mine
    for b in range(4):
        fs[c, b, :, 1536:1664] = sf[0, 12 * b : 12 * b + 16].astype(BF16)

    for e in (0, 1):
        core = c if e == 0 else oc
        for d in range(4):
            if e == 0 and d == 0:
                continue
            send(fs.at[core, xd(d)], r3.at[e, d], r3_send.at[e], r3_recv.at[e],
                 dev(core, z, y, xd(d)))

    await_bytes(dnr, misc_recv.at[6])

    def input_rows(i, _):
        rows = pl.ds(pl.multiple_of(i * 32, 32), 32)
        average, inverse = stat[0, rows, 0:1], stat[1, rows, 0:1]
        xhat = (x_vm[rows, :].astype(F32) - average) * inverse
        grad = dno[rows, :] + dnr[rows, :].astype(F32)
        m1 = jnp.mean(grad, axis=-1, keepdims=True)
        m2 = jnp.mean(grad * xhat, axis=-1, keepdims=True)
        gx_ref[0, rows, :] = (inverse * (grad - m1 - xhat * m2)).astype(BF16)
        return 0

    lax.fori_loop(0, ROWS // 32, input_rows, 0)

    await_bytes(r3.at[0, 1:4], r3_recv.at[0])
    await_bytes(r3.at[1], r3_recv.at[1])
    r3[0, 0] = fs[c, x]
    squares = jnp.zeros((12, 128), F32)
    for e in (0, 1):
        core = c if e == 0 else oc
        for i in range(2 * NC):
            total = r3[e, 0, :, i * 128 : (i + 1) * 128].astype(F32)
            for d in range(1, 4):
                total = total + r3[e, d, :, i * 128 : (i + 1) * 128].astype(F32)
            total = total[0:12]
            squares = squares + total * total
            at = pl.multiple_of((i % 2) * D + core * H + (i // 2) * CH, CH)
            gin_ref[:, pl.ds(at, CH)] = total
    total = r3[0, 0, :, 1536:1664].astype(F32)
    for d in range(1, 4):
        total = total + r3[0, d, :, 1536:1664].astype(F32)
    tap_rows = total[0:12]
    squares = squares + tap_rows * tap_rows

    part = jnp.sum(jnp.sum(squares, axis=0, keepdims=True), axis=1, keepdims=True)
    ps_s[0] = jnp.broadcast_to(part, (8, 128))
    count = 0
    for e in (0, 1):
        for d in range(4):
            if e == 0 and d == 0:
                continue
            send(ps_s.at[0], ps_r.at[count], ps_send.at[0], ps_recv.at[0],
                 dev(c if e == 0 else oc, z, y, xd(d)))
            count += 1
    await_bytes(ps_r.at[0:7], ps_recv.at[0])
    total = ps_s[0]
    for i in range(7):
        total = total + ps_r[i]
    ps_s[1] = total
    for d in (1, 2, 3):
        send(ps_s.at[1], ps_r.at[6 + d], ps_send.at[1], ps_recv.at[1], dev(c, z, yd(d), x))
    await_bytes(ps_r.at[7:10], ps_recv.at[1])
    total = ps_s[1] + ps_r[7] + ps_r[8] + ps_r[9]
    ps_s[2] = total
    for d in (1, 2, 3):
        send(ps_s.at[2], ps_r.at[9 + d], ps_send.at[2], ps_recv.at[2], dev(c, zd(d), y, x))
    await_bytes(ps_r.at[10:13], ps_recv.at[2])
    total = ps_s[2] + ps_r[10] + ps_r[11] + ps_r[12]
    msq = total[0:1, 0:1] / jnp.float32(2 * D * D + D * KT)
    scale = 1.0 / jnp.maximum(jnp.float32(1.0), jnp.sqrt(msq))
    gin_ref[...] = gin_ref[...] * scale
    gtap_ref[...] = (tap_rows * scale)[:, 0:KT]

    for j in range(NC):
        await_bytes(w_vm.at[j, pl.ds(0, H)], w_send.at[j])
        for part in (0, 1):
            await_bytes(r1.at[j, part], r1_send.at[j, part])
            await_bytes(r2.at[j, part], r2_send.at[j, part])
    await_bytes(cot_sib, misc_send.at[0])
    await_bytes(cot_halo, misc_send.at[1])
    await_bytes(tap_in, misc_send.at[2])
    await_bytes(halo.at[c], misc_send.at[3])
    await_bytes(na.at[own_rows], misc_send.at[4])
    await_bytes(halo.at[c], misc_send.at[5])
    await_bytes(dns, misc_send.at[6])
    for i in range(3):
        await_bytes(fb_r.at[i], fb_send.at[i])
    await_bytes(r3.at[0, 1:4], r3_send.at[0])
    await_bytes(r3.at[1], r3_send.at[1])
    await_bytes(t_r1, t_send.at[0])
    await_bytes(t_r2, t_send.at[1])
    await_bytes(ps_r.at[0:7], ps_send.at[0])
    await_bytes(ps_r.at[7:10], ps_send.at[1])
    await_bytes(ps_r.at[10:13], ps_send.at[2])


def body(activations, cotangent, lengths, poison, w_in, taps):
    vmem = pltpu.VMEM
    dma = pltpu.SemaphoreType.DMA
    scratch = [
        vmem((ROWS, D), BF16),
        vmem((ROWS, D), BF16),
        vmem((ROWS, H), BF16),
        vmem((2, 2, 16, H), BF16),
        vmem((ROWS, D), BF16),
        vmem((2, 2, 32, D), BF16),
        vmem((640, D), BF16),
        vmem((D, 512), BF16),
        vmem((NC, D, 2 * CH), BF16),
        vmem((2, ROWS, H), BF16),
        vmem((128, H), BF16),
        vmem((KT, H), BF16),
        vmem((KT, H), F32),
        vmem((KT, 8, CH), F32),
        vmem((640, 128), F32),
        vmem((2, ROWS, 128), F32),
        vmem((640, 2 * CH), F32),
        vmem((512, CH), F32),
        vmem((512, CH), F32),
        vmem((2, 64, 8, CH), F32),
        vmem((48, 8, CH), F32),
        vmem((2, 64, 8, CH), F32),
        vmem((16, 8, CH), F32),
        vmem((512, 2 * CH), BF16),
        vmem((NC, 512, 2 * CH), BF16),
        vmem((NC, 128, CH), F32),
        vmem((H, 128), BF16),
        vmem((NC, 2, 2, 4, 4, 48, CH), BF16),
        vmem((NC, 2, 3, 2, 4, 48, CH), BF16),
        vmem((NC, 2, 2, 4, 48, CH), BF16),
        vmem((NC, 2, 3, 2, 48, CH), BF16),
        vmem((2, 4, 16, 1664), BF16),
        vmem((2, 4, 16, 1664), BF16),
        vmem((2, 56, CH), F32),
        vmem((3, 192, 128), BF16),
        vmem((192, 128), BF16),
        vmem((3, 48, 128), BF16),
        vmem((ROWS, D), F32),
        vmem((ROWS, D), BF16),
        vmem((ROWS, D), BF16),
        vmem((3, 8, 128), jnp.int32),
        vmem((3, 3, 8, 128), jnp.int32),
        vmem((3, 8, 128), F32),
        vmem((13, 8, 128), F32),
        dma((2,)),
        dma((NC,)), dma((NC,)), dma((NC, 2)),
        dma((7,)), dma((7,)),
        dma((3,)), dma((3,)),
        dma((NC, 2)), dma((NC, 2)),
        dma((NC, 2)), dma((NC, 2)),
        dma((2,)), dma((2,)),
        dma((2,)), dma((2,)),
        dma((3,)), dma((3,)),
    ]
    anywhere = pl.BlockSpec(memory_space=pl.ANY)
    in_vmem = pl.BlockSpec(memory_space=pltpu.VMEM)
    in_smem = pl.BlockSpec(memory_space=pltpu.SMEM)
    return pl.pallas_call(
        kernel,
        out_shape=(
            jax.ShapeDtypeStruct((1, ROWS, D), BF16),
            jax.ShapeDtypeStruct((12, 2 * D), F32),
            jax.ShapeDtypeStruct((12, KT), F32),
        ),
        in_specs=[in_smem, in_smem, in_vmem, anywhere, anywhere, anywhere],
        out_specs=(in_vmem, in_vmem, in_vmem),
        scratch_shapes=scratch,
        compiler_params=pltpu.CompilerParams(
            collective_id=0, has_side_effects=True, vmem_limit_bytes=56 * 1024 * 1024
        ),
        name="conformer_conv",
    )(lengths, poison, taps.T, activations, cotangent, w_in)


def solution(mesh):
    placed = (
        P(("dp", "fsdp"), "seq", None),
        P(("dp", "fsdp"), "seq", None),
        P(("dp", "fsdp")),
        P(("dp", "fsdp"), "seq"),
        P("fsdp", None),
        P("fsdp", None),
    )
    return jax.shard_map(
        body,
        mesh=mesh,
        in_specs=placed,
        out_specs=(
            P(("dp", "fsdp"), "seq", None),
            P(("dp", "seq", "fsdp"), None),
            P(("dp", "seq", "fsdp"), None),
        ),
        check_vma=False,
    )
```

time: 1040 us -> 107 us (0.10)
  blocking collectives: 497 us -> 0 us
  waiting for transfers between devices: 233 us -> 0 us
  starting transfers between devices: 146 us -> 0 us
  Pallas kernels: 0 us -> 98.3 us
  local copies, waits for them, and re-layouts: 91.5 us -> 4.97 us
  other arithmetic: 31.1 us -> 0 us
  matrix products: 20.7 us -> 0 us
  between operations: 19.7 us -> 1.93 us
    unnamed x1 -> x0, blocking collectives: 409 us -> none
    unnamed x33 -> x0, starting transfers between devices: 135 us -> none
    unnamed x35 -> x0, waiting for transfers between devices: 125 us -> none
    all_gather x1 -> x0, waiting for transfers between devices: 98.5 us -> none  [body(): w_piece = lax.all_gather(w_in, 'fsdp', axis=0, tiled=True)]
    pallas_call x0 -> x1, Pallas kernels: none -> 98.3 us  [body(): pl.pallas_call(kernel, out_shape=(jax.ShapeDtypeStruct((1, ROWS, D), BF16...]
    unnamed x183 -> x3, local copies, waits for them, and re-layouts: 88 us -> 4.97 us
    psum x1 -> x0, blocking collectives: 63.6 us -> none  [body(): total = lax.psum(local_sq, ('dp', 'seq', 'fsdp'))]
    dot_general x3 -> x0, matrix products: 20.7 us -> none  [the longest x1 8.11 us: body(): lax.dot_general(cols, dpre, (((0,), (0,)), ((), ())), preferred_element_t...]
  transfers between devices with their start and end apart: 38 -> 0, of which waited for: 10 -> 0; matrix products, arithmetic and copies ran while one was open for 2% -> 0% of each run, Pallas kernels for 0% -> 0%
where the time goes in v1:
time: 107 us; the launch traced here: 105 us
  Pallas kernels  98.3 us (92%)
  local copies, waits for them, and re-layouts  4.97 us (5%)
  between operations  1.93 us (2%)
    pallas_call x1, Pallas kernels, body(): pl.pallas_call(kernel, out_shape=(jax.ShapeDtypeStruct((1, ROWS, D), BF16...  98.3 us
    unnamed x3, local copies, waits for them, and re-layouts  4.97 us

profile of v1, /device:TPU:1, one launch (start us, length us, event | category | flops | bytes accessed | tf_op | source)
XLA Modules:
  0.0 105.2 jit_solution(11158846841952826706)
XLA Ops:
  1.9 98.3 %conformer_conv.1 = (bf16[1,256,1536]{2,1,0:T(8,128)(2,1)}, f32[12,3072]{1,0:T(8,128)}, f32[12,32]{1,0:T(8,128)}) custom-call(s32[1]{0:T(128)S(6)} %copy.12.len_ref, s32[1,1]{1,0:T(1,128)S(6)} %copy.13.poi_ref, bf16[32,768]{1,0:T(8,128)(2,1)} %bitcast.1, bf16[1,256,1536]{2,1,0:T(8,128)(2,1)} %x_hbm.1, bf16[1,256,1536]{2,1,0:T(8,128)(2,1)} %cot_hbm.1, ...), custom_call_target="tpu_custom_call" | custom-call | tf_op jit(solution)/shard_map/conformer_conv/pallas_call | solution.py:637
  100.3 2.1 %copy.14 = bf16[1,256,1536]{2,1,0:T(8,128)(2,1)} copy(bf16[1,256,1536]{2,1,0:T(8,128)(2,1)} %get-tuple-element.6) | data formatting | bytes 1572864
  102.3 1.6 %copy.15 = f32[12,3072]{1,0:T(8,128)} copy(f32[12,3072]{1,0:T(8,128)} %get-tuple-element.7) | data formatting | bytes 294912
  103.9 1.3 %copy.16 = f32[12,32]{1,0:T(8,128)} copy(f32[12,32]{1,0:T(8,128)} %get-tuple-element.8) | data formatting | bytes 3072

commit v2 on v1

--- a/solution.py
+++ b/solution.py
@@ -43,11 +43,11 @@
 
 def kernel(
     len_ref, poi_ref, taps_ref, x_hbm, cot_hbm, w_hbm,
-    gx_ref, gin_ref, gtap_ref,
-    x_vm, cot_vm, cot_sib, cot_halo, nn, halo, na, nt, w_vm, cp, cph,
-    tap_in, tapf, tb, msk, stat, pre, val_s, sig_s, xe, xh, de, dh, dp, dpn,
+    gx_hbm, gin_hbm, gtap_hbm,
+    x_vm, cot_vm, cot_sib, cot_halo, edges, nn, halo, na, nt, w_vm, cp, cph,
+    tap_in, tapf, tb, msk, keep, stat, pre, val_s, sig_s, xe, xh, de, dh, dp, dpn,
     tg, tt, g, r1, s1, r2, fs, r3, sf, t_r1, t_s1, t_r2,
-    dno, dns, dnr, fb_s, fb_r, ps_s, ps_r,
+    dno, dns, dnr, gx_vm, gin_vm, gtap_vm, fb_s, fb_r, ps_s, ps_r,
     local_sem, w_loc, w_send, w_recv, misc_send, misc_recv, fb_send, fb_recv,
     r1_send, r1_recv, r2_send, r2_recv, r3_send, r3_recv, t_send, t_recv, ps_send, ps_recv,
 ):
@@ -123,7 +123,7 @@
             base = pl.multiple_of((1 - f) * H + side * (H // 2), H // 2)
             await_bytes(w_vm.at[j, pl.ds(base, H // 2)], w_recv.at[j, side])
 
-    for j in range(2):
+    for j in range(NC):
         local_w(j)
 
     frame0 = s * ROWS
@@ -142,7 +142,8 @@
 
     pl.semaphore_wait(barrier, len(partners))
 
-    send_w(0)
+    send(x_hbm.at[0, pl.ds(ROWS - 32, 32)], edges.at[0], misc_send.at[3], misc_recv.at[3], (c, nxt, f))
+    send(x_hbm.at[0, pl.ds(0, 32)], edges.at[1], misc_send.at[3], misc_recv.at[3], (c, prv, f))
     for k, partner in enumerate((sibling, dev(c, z, y, xd(2)), dev(oc, z, y, xd(2)))):
         send(fb_s.at[0], fb_r.at[0, k], fb_send.at[0], fb_recv.at[0], partner)
     send(
@@ -156,24 +157,26 @@
         send(cot_vm.at[pl.ds(0, 16), cols], cot_halo.at[c, 1],
              misc_send.at[1], misc_recv.at[1], (e, prv, f))
     send(taps_ref, tap_in, misc_send.at[2], misc_recv.at[2], dev(c, z, y, xd(3)))
-    send_w(1)
+    for j in range(NC):
+        send_w(j)
 
     load_x.wait()
 
-    def norm_rows(i, _):
-        rows = pl.ds(pl.multiple_of(i * 32, 32), 32)
-        xf = x_vm[rows, :].astype(F32)
+    def normalised(frames):
+        xf = frames.astype(F32)
         average = jnp.mean(xf, axis=-1, keepdims=True)
         cent = xf - average
         inverse = lax.rsqrt(jnp.mean(cent * cent, axis=-1, keepdims=True) + 1e-05)
-        nn[rows, :] = (cent * inverse).astype(BF16)
+        return (cent * inverse).astype(BF16), average, inverse
+
+    def norm_rows(i, _):
+        rows = pl.ds(pl.multiple_of(i * 32, 32), 32)
+        nn[rows, :], average, inverse = normalised(x_vm[rows, :])
         stat[0, rows, :] = jnp.broadcast_to(average, (32, 128))
         stat[1, rows, :] = jnp.broadcast_to(inverse, (32, 128))
         return 0
 
     lax.fori_loop(0, ROWS // 32, norm_rows, 0)
-    send(nn.at[pl.ds(ROWS - 32, 32)], halo.at[c, 0], misc_send.at[3], misc_recv.at[3], (c, nxt, f))
-    send(nn.at[pl.ds(0, 32)], halo.at[c, 1], misc_send.at[3], misc_recv.at[3], (c, prv, f))
 
     r0, r1i = iota((ROWS, ROWS), 0), iota((ROWS, ROWS), 1)
     to_phase = one_hot((r0 % 8) * 32 + r0 // 8 == r1i)
@@ -191,7 +194,9 @@
         cols = pl.ds(i * 128, 128)
         nt[cols, own_rows] = na[own_rows, cols].T
 
-    await_bytes(halo.at[c], misc_recv.at[3])
+    await_bytes(edges, misc_recv.at[3])
+    for side in (0, 1):
+        halo[c, side] = normalised(edges[side])[0]
     send(halo.at[c], halo.at[c], misc_send.at[5], misc_recv.at[5], sibling)
 
     await_bytes(fb_r.at[1], fb_recv.at[1])
@@ -213,48 +218,33 @@
     halo_order = one_hot(source == h1)
     na[512:640, :] = dot(halo_order, halo[...].reshape(128, D)).astype(BF16)
 
-    await_bytes(fb_r.at[2], fb_recv.at[2])
-    votes = jnp.minimum(jnp.minimum(fb_s[2], fb_r[2, 0]), jnp.minimum(fb_r[2, 1], fb_r[2, 2]))
     await_bytes(cot_sib, misc_recv.at[0])
-    await_bytes(cot_halo, misc_recv.at[1])
-    ra = iota((ROWS, 128), 0)
-    frame = frame0 + (ra % 8) * 32 + ra // 8
-    for own in (True, False):
-        if own:
-            part = cot_vm[:, pl.ds(pl.multiple_of(c * H, H), H)]
-            u = c
-        else:
-            part = cot_sib[...]
-            u = oc
-        first = jnp.min(
-            jnp.where(iota((8, 128), 0) == u, votes, jnp.int32(BIG)), axis=0, keepdims=True
-        )
-        keep = jnp.where(frame < first, jnp.float32(1.0), jnp.float32(0.0))
-        moved = dot(to_phase, part)
-        for i in range(NC):
-            cp[u, :, i * CH : (i + 1) * CH] = (moved[:, i * CH : (i + 1) * CH] * keep).astype(BF16)
+    cp[c] = dot(to_phase, cot_vm[:, pl.ds(pl.multiple_of(c * H, H), H)]).astype(BF16)
+    cp[oc] = dot(to_phase, cot_sib[...]).astype(BF16)
     c0, c1 = iota((128, 64), 0), iota((128, 64), 1)
     edge_order = one_hot(
         jnp.logical_and(c0 % 8 < 4, (c0 % 8) * 16 + c0 // 8 == c1)
     )
+    await_bytes(cot_halo, misc_recv.at[1])
+    cph[...] = dot(edge_order, cot_halo[...].reshape(64, H)).astype(BF16)
+
+    ra = iota((ROWS, 128), 0)
+    frame = frame0 + (ra % 8) * 32 + ra // 8
     hr = iota((128, 128), 0)
     place, q = hr % 8, hr // 8
-    edge_frame = frame0 + jnp.where(place % 2 == 0, q - 16, q + ROWS)
-    limit = jnp.where((place // 2) % 2 == 0, votes[0:1], votes[1:2])
-    keep = jnp.logical_and(edge_frame >= 0, edge_frame < limit)
-    keep = jnp.where(keep, jnp.float32(1.0), jnp.float32(0.0))
-    moved = dot(edge_order, cot_halo[...].reshape(64, H))
-    for i in range(NC):
-        cph[:, i * CH : (i + 1) * CH] = (moved[:, i * CH : (i + 1) * CH] * keep).astype(BF16)
-
-    for u in (0, 1):
-        msk[u * ROWS : (u + 1) * ROWS, :] = jnp.where(
-            frame < votes[2 + u : 3 + u], jnp.float32(1.0), jnp.float32(0.0)
-        )
-    halo_frame = frame0 + jnp.where(place % 2 == 0, q - 32, q + ROWS) + (place // 4) * 16
-    limit = jnp.where((place // 2) % 2 == 0, votes[2:3], votes[3:4])
-    keep = jnp.logical_and(halo_frame >= 0, halo_frame < limit)
-    msk[512:640, :] = jnp.where(keep, jnp.float32(1.0), jnp.float32(0.0))
+    first_half = jnp.where(place % 2 == 0, q - 16, q + ROWS) + frame0
+    halo_frame = jnp.where(place % 2 == 0, q - 32, q + ROWS) + (place // 4) * 16 + frame0
+
+    def valid(flag):
+        return jnp.where(flag, jnp.float32(1.0), jnp.float32(0.0))
+
+    def masks(out, limits, edge):
+        for u in (0, 1):
+            out[u * ROWS : (u + 1) * ROWS, :] = valid(frame < limits[u : u + 1])
+        limit = jnp.where((place // 2) % 2 == 0, limits[0:1], limits[1:2])
+        out[512:640, :] = valid(jnp.logical_and(edge >= 0, edge < limit))
+
+    masks(msk, fb_s[1, 2:4], halo_frame)
 
     from_phase = one_hot((r1i % 8) * 32 + r1i // 8 == r0)
 
@@ -288,29 +278,53 @@
     def stage2_finish(j):
         for part in (0, 1):
             await_bytes(r2.at[j, part], r2_recv.at[j, part])
-            lanes = pl.ds(pl.multiple_of(j * 256 + part * 128, 128), 128)
+            lanes = pl.ds(pl.multiple_of((j % 2) * 256 + part * 128, 128), 128)
             for a in (0, 1):
                 total = s1[j, part, a, y if part == 0 else z].astype(F32)
                 for d in range(3):
                     total = total + r2[j, part, d, a].astype(F32)
                 sf[a, 0:48] = total
                 for b in range(4):
-                    fs[a, b, :, lanes] = sf[a, 12 * b : 12 * b + 16].astype(BF16)
+                    fs[j // 2, a, b, :, lanes] = sf[a, 12 * b : 12 * b + 16].astype(BF16)
+
+    def stage3_start(q, width):
+        for e in (0, 1):
+            core = c if e == 0 else oc
+            for d in range(4):
+                if e == 0 and d == 0:
+                    continue
+                send(fs.at[q, core, xd(d), :, pl.ds(0, width)], r3.at[q, e, d, :, pl.ds(0, width)],
+                     r3_send.at[q, e], r3_recv.at[q, e], dev(core, z, y, xd(d)))
+
+    def stage3_await(q, width, sems):
+        await_bytes(r3.at[q, 0, 1:4, :, pl.ds(0, width)], sems.at[q, 0])
+        await_bytes(r3.at[q, 1, :, :, pl.ds(0, width)], sems.at[q, 1])
+
+    def stage3_finish(q, width):
+        stage3_await(q, width, r3_recv)
+        r3[q, 0, 0] = fs[q, c, x]
+        squares = jnp.zeros((12, 128), F32)
+        for e in (0, 1):
+            core = c if e == 0 else oc
+            for i in range(4):
+                total = r3[q, e, 0, :, i * 128 : (i + 1) * 128].astype(F32)
+                for d in range(1, 4):
+                    total = total + r3[q, e, d, :, i * 128 : (i + 1) * 128].astype(F32)
+                total = total[0:12]
+                squares = squares + total * total
+                at = pl.multiple_of((i % 2) * D + core * H + (2 * q + i // 2) * CH, CH)
+                gin_vm[:, pl.ds(at, CH)] = total
+        return squares
 
     sf[...] = jnp.zeros_like(sf)
     tg[...] = jnp.zeros_like(tg)
     for a in (0, 1):
         for b in range(4):
-            fs[a, b, :, 1536:1664] = jnp.zeros((16, 128), BF16)
+            fs[2, a, b, :, 512:640] = jnp.zeros((16, 128), BF16)
 
     sub = iota((16, 8, 128), 1)
 
     def chunk(j, _):
-        @pl.when(j + 2 < NC)
-        def _():
-            local_w(j + 2)
-            send_w(j + 2)
-
         lanes = pl.ds(pl.multiple_of(j * CH, CH), CH)
         for k in range(KT):
             tb[k] = jnp.broadcast_to(tapf[k : k + 1, lanes], (8, 128))
@@ -360,14 +374,24 @@
             u, b = i // 4, i % 4
             total = conv(xe[u, pl.ds(b * 8, 39)])
             cot = cp[u, pl.ds(pl.multiple_of(b * 64, 64), 64), lanes].astype(F32)
+            cot = cot * keep[pl.ds(pl.multiple_of(i * 64, 64), 64), :]
             de[u, pl.ds(16 + b * 8, 8)] = through_swish(total, cot.reshape(8, 8, CH))
             return 0
+
+        @pl.when(j == 0)
+        def _():
+            await_bytes(fb_r.at[2], fb_recv.at[2])
+            votes = jnp.minimum(
+                jnp.minimum(fb_s[2], fb_r[2, 0]), jnp.minimum(fb_r[2, 1], fb_r[2, 2])
+            )
+            masks(keep, votes, first_half)
 
         lax.fori_loop(0, 8, forward, 0)
 
         def forward_edge(b, _):
             total = conv(xh[pl.ds(b * 8, 39)])
             cot = cph[pl.ds(pl.multiple_of(b * 64, 64), 64), lanes].astype(F32)
+            cot = cot * keep[pl.ds(pl.multiple_of(512 + b * 64, 64), 64), :]
             dh[pl.ds(b * 8, 8)] = through_swish(total, cot.reshape(8, 8, CH))
             return 0
 
@@ -425,6 +449,10 @@
         def _():
             stage2_finish(j - 2)
 
+        @pl.when(jnp.logical_and(j >= 3, j % 2 == 1))
+        def _():
+            stage3_start((j - 3) // 2, 512)
+
         return 0
 
     lax.fori_loop(0, NC, chunk, 0)
@@ -477,15 +505,9 @@
         mine = mine + t_r2[d].astype(F32)
     sf[0, 0:48] = mine
     for b in range(4):
-        fs[c, b, :, 1536:1664] = sf[0, 12 * b : 12 * b + 16].astype(BF16)
-
-    for e in (0, 1):
-        core = c if e == 0 else oc
-        for d in range(4):
-            if e == 0 and d == 0:
-                continue
-            send(fs.at[core, xd(d)], r3.at[e, d], r3_send.at[e], r3_recv.at[e],
-                 dev(core, z, y, xd(d)))
+        fs[2, c, b, :, 512:640] = sf[0, 12 * b : 12 * b + 16].astype(BF16)
+
+    stage3_start(2, 640)
 
     await_bytes(dnr, misc_recv.at[6])
 
@@ -496,28 +518,17 @@
         grad = dno[rows, :] + dnr[rows, :].astype(F32)
         m1 = jnp.mean(grad, axis=-1, keepdims=True)
         m2 = jnp.mean(grad * xhat, axis=-1, keepdims=True)
-        gx_ref[0, rows, :] = (inverse * (grad - m1 - xhat * m2)).astype(BF16)
+        gx_vm[rows, :] = (inverse * (grad - m1 - xhat * m2)).astype(BF16)
         return 0
 
     lax.fori_loop(0, ROWS // 32, input_rows, 0)
-
-    await_bytes(r3.at[0, 1:4], r3_recv.at[0])
-    await_bytes(r3.at[1], r3_recv.at[1])
-    r3[0, 0] = fs[c, x]
-    squares = jnp.zeros((12, 128), F32)
-    for e in (0, 1):
-        core = c if e == 0 else oc
-        for i in range(2 * NC):
-            total = r3[e, 0, :, i * 128 : (i + 1) * 128].astype(F32)
-            for d in range(1, 4):
-                total = total + r3[e, d, :, i * 128 : (i + 1) * 128].astype(F32)
-            total = total[0:12]
-            squares = squares + total * total
-            at = pl.multiple_of((i % 2) * D + core * H + (i // 2) * CH, CH)
-            gin_ref[:, pl.ds(at, CH)] = total
-    total = r3[0, 0, :, 1536:1664].astype(F32)
+    store_gx = pltpu.make_async_copy(gx_vm, gx_hbm.at[0], local_sem.at[0])
+    store_gx.start()
+
+    squares = stage3_finish(0, 512) + stage3_finish(1, 512) + stage3_finish(2, 640)
+    total = r3[2, 0, 0, :, 512:640].astype(F32)
     for d in range(1, 4):
-        total = total + r3[0, d, :, 1536:1664].astype(F32)
+        total = total + r3[2, 0, d, :, 512:640].astype(F32)
     tap_rows = total[0:12]
     squares = squares + tap_rows * tap_rows
 
@@ -547,8 +558,12 @@
     total = ps_s[2] + ps_r[10] + ps_r[11] + ps_r[12]
     msq = total[0:1, 0:1] / jnp.float32(2 * D * D + D * KT)
     scale = 1.0 / jnp.maximum(jnp.float32(1.0), jnp.sqrt(msq))
-    gin_ref[...] = gin_ref[...] * scale
-    gtap_ref[...] = (tap_rows * scale)[:, 0:KT]
+    gin_vm[...] = gin_vm[...] * scale
+    gtap_vm[...] = (tap_rows * scale)[:, 0:KT]
+    store_gin = pltpu.make_async_copy(gin_vm, gin_hbm, local_sem.at[1])
+    store_gin.start()
+    store_gtap = pltpu.make_async_copy(gtap_vm, gtap_hbm, local_sem.at[2])
+    store_gtap.start()
 
     for j in range(NC):
         await_bytes(w_vm.at[j, pl.ds(0, H)], w_send.at[j])
@@ -558,19 +573,28 @@
     await_bytes(cot_sib, misc_send.at[0])
     await_bytes(cot_halo, misc_send.at[1])
     await_bytes(tap_in, misc_send.at[2])
-    await_bytes(halo.at[c], misc_send.at[3])
+    await_bytes(edges, misc_send.at[3])
     await_bytes(na.at[own_rows], misc_send.at[4])
     await_bytes(halo.at[c], misc_send.at[5])
     await_bytes(dns, misc_send.at[6])
     for i in range(3):
         await_bytes(fb_r.at[i], fb_send.at[i])
-    await_bytes(r3.at[0, 1:4], r3_send.at[0])
-    await_bytes(r3.at[1], r3_send.at[1])
+    for q, width in ((0, 512), (1, 512), (2, 640)):
+        stage3_await(q, width, r3_send)
     await_bytes(t_r1, t_send.at[0])
     await_bytes(t_r2, t_send.at[1])
     await_bytes(ps_r.at[0:7], ps_send.at[0])
     await_bytes(ps_r.at[7:10], ps_send.at[1])
     await_bytes(ps_r.at[10:13], ps_send.at[2])
+    store_gx.wait()
+    store_gin.wait()
+    store_gtap.wait()
+
+
+def hand_over(gx, gin, gtap, gx_out, gin_out, gtap_out):
+    gx_out[...] = gx[...]
+    gin_out[...] = gin[...]
+    gtap_out[...] = gtap[...]
 
 
 def body(activations, cotangent, lengths, poison, w_in, taps):
@@ -581,6 +605,7 @@
         vmem((ROWS, D), BF16),
         vmem((ROWS, H), BF16),
         vmem((2, 2, 16, H), BF16),
+        vmem((2, 32, D), BF16),
         vmem((ROWS, D), BF16),
         vmem((2, 2, 32, D), BF16),
         vmem((640, D), BF16),
@@ -591,6 +616,7 @@
         vmem((KT, H), BF16),
         vmem((KT, H), F32),
         vmem((KT, 8, CH), F32),
+        vmem((640, 128), F32),
         vmem((640, 128), F32),
         vmem((2, ROWS, 128), F32),
         vmem((640, 2 * CH), F32),
@@ -608,8 +634,8 @@
         vmem((NC, 2, 3, 2, 4, 48, CH), BF16),
         vmem((NC, 2, 2, 4, 48, CH), BF16),
         vmem((NC, 2, 3, 2, 48, CH), BF16),
-        vmem((2, 4, 16, 1664), BF16),
-        vmem((2, 4, 16, 1664), BF16),
+        vmem((3, 2, 4, 16, 640), BF16),
+        vmem((3, 2, 4, 16, 640), BF16),
         vmem((2, 56, CH), F32),
         vmem((3, 192, 128), BF16),
         vmem((192, 128), BF16),
@@ -617,38 +643,49 @@
         vmem((ROWS, D), F32),
         vmem((ROWS, D), BF16),
         vmem((ROWS, D), BF16),
+        vmem((ROWS, D), BF16),
+        vmem((12, 2 * D), F32),
+        vmem((12, KT), F32),
         vmem((3, 8, 128), jnp.int32),
         vmem((3, 3, 8, 128), jnp.int32),
         vmem((3, 8, 128), F32),
         vmem((13, 8, 128), F32),
-        dma((2,)),
+        dma((3,)),
         dma((NC,)), dma((NC,)), dma((NC, 2)),
         dma((7,)), dma((7,)),
         dma((3,)), dma((3,)),
         dma((NC, 2)), dma((NC, 2)),
         dma((NC, 2)), dma((NC, 2)),
-        dma((2,)), dma((2,)),
+        dma((3, 2)), dma((3, 2)),
         dma((2,)), dma((2,)),
         dma((3,)), dma((3,)),
     ]
     anywhere = pl.BlockSpec(memory_space=pl.ANY)
     in_vmem = pl.BlockSpec(memory_space=pltpu.VMEM)
     in_smem = pl.BlockSpec(memory_space=pltpu.SMEM)
-    return pl.pallas_call(
+    shapes = (
+        jax.ShapeDtypeStruct((1, ROWS, D), BF16),
+        jax.ShapeDtypeStruct((12, 2 * D), F32),
+        jax.ShapeDtypeStruct((12, KT), F32),
+    )
+    results = pl.pallas_call(
         kernel,
-        out_shape=(
-            jax.ShapeDtypeStruct((1, ROWS, D), BF16),
-            jax.ShapeDtypeStruct((12, 2 * D), F32),
-            jax.ShapeDtypeStruct((12, KT), F32),
-        ),
+        out_shape=shapes,
         in_specs=[in_smem, in_smem, in_vmem, anywhere, anywhere, anywhere],
-        out_specs=(in_vmem, in_vmem, in_vmem),
+        out_specs=(anywhere, anywhere, anywhere),
         scratch_shapes=scratch,
         compiler_params=pltpu.CompilerParams(
             collective_id=0, has_side_effects=True, vmem_limit_bytes=56 * 1024 * 1024
         ),
         name="conformer_conv",
     )(lengths, poison, taps.T, activations, cotangent, w_in)
+    return pl.pallas_call(
+        hand_over,
+        out_shape=shapes,
+        in_specs=[in_vmem] * 3,
+        out_specs=(in_vmem,) * 3,
+        name="hand_over",
+    )(*results)
 
 
 def solution(mesh):

time: 107 us -> 90.9 us (0.85)
  Pallas kernels: 98.3 us -> 88 us
  local copies, waits for them, and re-layouts: 4.97 us -> 0 us
    pallas_call x1 -> x2, Pallas kernels: 98.3 us -> 88 us  [the longest x1 85.8 us: body(): pl.pallas_call(kernel, out_shape=shapes, in_specs=[in_smem, in_smem, in_v...]
    unnamed x3 -> x0, local copies, waits for them, and re-layouts: 4.97 us -> none
where the time goes in v2:
time: 90.9 us; the launch traced here: 89.9 us
  Pallas kernels  88 us (97%)
  between operations  1.93 us (2%)
    pallas_call x1, Pallas kernels, body(): pl.pallas_call(kernel, out_shape=shapes, in_specs=[in_smem, in_smem, in_v...  85.8 us
    pallas_call x1, Pallas kernels, body(): pl.pallas_call(hand_over, out_shape=shapes, in_specs=[in_vmem] * 3, out_s...  2.21 us

profile of v2, /device:TPU:1, one launch (start us, length us, event | category | flops | bytes accessed | tf_op | source)
XLA Modules:
  0.0 89.9 jit_solution(5509657371096157780)
XLA Ops:
  1.9 85.8 %conformer_conv.1 = (bf16[1,256,1536]{2,1,0:T(8,128)(2,1)}, f32[12,3072]{1,0:T(8,128)}, f32[12,32]{1,0:T(8,128)}) custom-call(s32[1]{0:T(128)S(6)} %copy.9.len_ref, s32[1,1]{1,0:T(1,128)S(6)} %copy.10.poi_ref, bf16[32,768]{1,0:T(8,128)(2,1)} %bitcast.1, bf16[1,256,1536]{2,1,0:T(8,128)(2,1)} %x_hbm.1, bf16[1,256,1536]{2,1,0:T(8,128)(2,1)} %cot_hbm.1, ...), custom_call_target="tpu_custom_call" | custom-call | tf_op jit(solution)/shard_map/conformer_conv/pallas_call | solution.py:671
  87.7 2.2 %hand_over.1 = (bf16[1,256,1536]{2,1,0:T(8,128)(2,1)}, f32[12,3072]{1,0:T(8,128)}, f32[12,32]{1,0:T(8,128)}) custom-call(bf16[1,256,1536]{2,1,0:T(8,128)(2,1)} %get-tuple-element.6.gx, f32[12,3072]{1,0:T(8,128)} %get-tuple-element.7.gin, f32[12,32]{1,0:T(8,128)} %get-tuple-element.8.gtap), custom_call_target="tpu_custom_call" | custom-call | tf_op jit(solution)/shard_map/hand_over/pallas_call | solution.py:682

commit v3 on v2

--- a/solution.py
+++ b/solution.py
@@ -46,10 +46,10 @@
     gx_hbm, gin_hbm, gtap_hbm,
     x_vm, cot_vm, cot_sib, cot_halo, edges, nn, halo, na, nt, w_vm, cp, cph,
     tap_in, tapf, tb, msk, keep, stat, pre, val_s, sig_s, xe, xh, de, dh, dp, dpn,
-    tg, tt, g, r1, s1, r2, fs, r3, sf, t_r1, t_s1, t_r2,
+    tg, tt, g, rd, s1, r2, fs, r3, sf, t_r1, t_s1, t_r2,
     dno, dns, dnr, gx_vm, gin_vm, gtap_vm, fb_s, fb_r, ps_s, ps_r,
     local_sem, w_loc, w_send, w_recv, misc_send, misc_recv, fb_send, fb_recv,
-    r1_send, r1_recv, r2_send, r2_recv, r3_send, r3_recv, t_send, t_recv, ps_send, ps_recv,
+    rd_send, rd_recv, r2_send, r2_recv, r3_send, r3_recv, t_send, t_recv, ps_send, ps_recv,
 ):
     c = lax.axis_index("dp")
     s = lax.axis_index("seq")
@@ -142,10 +142,10 @@
 
     pl.semaphore_wait(barrier, len(partners))
 
+    for k, partner in enumerate((sibling, dev(c, z, y, xd(2)), dev(oc, z, y, xd(2)))):
+        send(fb_s.at[0], fb_r.at[0, k], fb_send.at[0], fb_recv.at[0], partner)
     send(x_hbm.at[0, pl.ds(ROWS - 32, 32)], edges.at[0], misc_send.at[3], misc_recv.at[3], (c, nxt, f))
     send(x_hbm.at[0, pl.ds(0, 32)], edges.at[1], misc_send.at[3], misc_recv.at[3], (c, prv, f))
-    for k, partner in enumerate((sibling, dev(c, z, y, xd(2)), dev(oc, z, y, xd(2)))):
-        send(fb_s.at[0], fb_r.at[0, k], fb_send.at[0], fb_recv.at[0], partner)
     send(
         cot_vm.at[:, pl.ds(pl.multiple_of(oc * H, H), H)], cot_sib,
         misc_send.at[0], misc_recv.at[0], sibling,
@@ -228,8 +228,8 @@
     await_bytes(cot_halo, misc_recv.at[1])
     cph[...] = dot(edge_order, cot_halo[...].reshape(64, H)).astype(BF16)
 
-    ra = iota((ROWS, 128), 0)
-    frame = frame0 + (ra % 8) * 32 + ra // 8
+    ri = iota((ROWS, 128), 0)
+    frame = frame0 + (ri % 8) * 32 + ri // 8
     hr = iota((128, 128), 0)
     place, q = hr % 8, hr // 8
     first_half = jnp.where(place % 2 == 0, q - 16, q + ROWS) + frame0
@@ -248,27 +248,32 @@
 
     from_phase = one_hot((r1i % 8) * 32 + r1i // 8 == r0)
 
-    def stage1_start(j):
-        for d in (1, 2, 3):
-            send(g.at[j, 0, :, zd(d)], r1.at[j, 0, d - 1], r1_send.at[j, 0], r1_recv.at[j, 0],
-                 dev(c, zd(d), y, x))
-            send(g.at[j, 1, :, :, yd(d)], r1.at[j, 1, d - 1], r1_send.at[j, 1], r1_recv.at[j, 1],
-                 dev(c, z, yd(d), x))
-
-    def stage1_finish(j):
+    def ring_dev(part, d):
+        return dev(c, zd(d), y, x) if part == 0 else dev(c, z, yd(d), x)
+
+    def direct_start(j):
         for part in (0, 1):
-            await_bytes(r1.at[j, part], r1_recv.at[j, part])
+            for d in (1, 2, 3):
+                src = g.at[j, 0, :, zd(d)] if part == 0 else g.at[j, 1, :, :, yd(d)]
+                send(src, rd.at[j, part, d - 1], rd_send.at[j, part], rd_recv.at[j, part], ring_dev(part, d))
+
+    def direct_finish(j):
+        for part in (0, 1):
+            await_bytes(rd.at[j, part], rd_recv.at[j, part])
 
             def add(i, _):
                 a, b = i // 4, i % 4
-                mine = g[j, 0, a, z, b] if part == 0 else g[j, 1, a, b, y]
-                total = mine.astype(F32)
+                own = g[j, 0, a, z, b] if part == 0 else g[j, 1, a, b, y]
+                total = own.astype(F32)
                 for d in range(3):
-                    total = total + r1[j, part, d, a, b].astype(F32)
+                    total = total + rd[j, part, d, a, b].astype(F32)
                 s1[j, part, a, b] = total.astype(BF16)
                 return 0
 
             lax.fori_loop(0, 8, add, 0)
+        stage2_start(j)
+
+    def stage2_start(j):
         for d in (1, 2, 3):
             send(s1.at[j, 0, :, yd(d)], r2.at[j, 0, d - 1], r2_send.at[j, 0], r2_recv.at[j, 0],
                  dev(c, z, yd(d), x))
@@ -386,7 +391,7 @@
             )
             masks(keep, votes, first_half)
 
-        lax.fori_loop(0, 8, forward, 0)
+        lax.fori_loop(0, 8, forward, 0, unroll=4)
 
         def forward_edge(b, _):
             total = conv(xh[pl.ds(b * 8, 39)])
@@ -418,32 +423,35 @@
             dp[rows, CH:] = (dval * val * (1.0 - sig)).astype(BF16)
             return 0
 
-        lax.fori_loop(0, 8, backward, 0)
-
-        def tap_terms(i, total):
-            u, b = i // 4, i % 4
-            window = xe[u, pl.ds(b * 8, 39)]
-            grads = de[u, pl.ds(16 + b * 8, 8)]
-            for m in range(8):
-                total = total + grads[m][None] * window[m : m + 32]
-            return total
-
-        terms = lax.fori_loop(0, 8, tap_terms, jnp.zeros((KT, 8, CH), F32))
-        tg[j, 0:KT] = jnp.sum(terms, axis=1)
+        lax.fori_loop(0, 8, backward, 0, unroll=4)
 
         for i in range(8):
             grad = dot(nt[i * 192 : (i + 1) * 192, :], dp[...])
             for part in (0, 1):
                 half = grad[:, part * CH : (part + 1) * CH].astype(BF16)
                 g[j, part, i // 4, i % 4] = half.reshape(4, 48, CH)
-        stage1_start(j)
+
+        direct_start(j)
+
+        for h in (0, 16):
+
+            def tap_terms(i, total):
+                u, b = i // 4, i % 4
+                window = xe[u, pl.ds(b * 8 + h, 23)]
+                grads = de[u, pl.ds(16 + b * 8, 8)]
+                for m in range(8):
+                    total = total + grads[m][None] * window[m : m + 16]
+                return total
+
+            terms = lax.fori_loop(0, 8, tap_terms, jnp.zeros((16, 8, CH), F32), unroll=4)
+            tg[j, h : h + 16] = jnp.sum(terms, axis=1)
         for u in (0, 1):
             rows = slice(u * ROWS, (u + 1) * ROWS)
             dpn[j, rows, :] = dot(from_phase, dp[rows, :]).astype(BF16)
 
         @pl.when(j >= 1)
         def _():
-            stage1_finish(j - 1)
+            direct_finish(j - 1)
 
         @pl.when(j >= 2)
         def _():
@@ -480,7 +488,7 @@
     lax.fori_loop(0, D // 256, sibling_part, 0)
     send(dns, dnr, misc_send.at[6], misc_recv.at[6], sibling)
 
-    stage1_finish(NC - 1)
+    direct_finish(NC - 1)
     stage2_finish(NC - 2)
     await_bytes(t_r1, t_recv.at[0])
     mine = tt[pl.ds(pl.multiple_of(z * 192, 16), 192), :].astype(F32)
@@ -568,8 +576,10 @@
     for j in range(NC):
         await_bytes(w_vm.at[j, pl.ds(0, H)], w_send.at[j])
         for part in (0, 1):
-            await_bytes(r1.at[j, part], r1_send.at[j, part])
             await_bytes(r2.at[j, part], r2_send.at[j, part])
+    for j in range(NC):
+        for part in (0, 1):
+            await_bytes(rd.at[j, part], rd_send.at[j, part])
     await_bytes(cot_sib, misc_send.at[0])
     await_bytes(cot_halo, misc_send.at[1])
     await_bytes(tap_in, misc_send.at[2])

time: 90.9 us -> 87.9 us (0.967)
  Pallas kernels: 88 us -> 85 us
    pallas_call x1, Pallas kernels: 85.8 us -> 82.8 us  [body(): pl.pallas_call(kernel, out_shape=shapes, in_specs=[in_smem, in_smem, in_v...]
where the time goes in v3:
time: 87.9 us; the launch traced here: 87 us
  Pallas kernels  85 us (97%)
  between operations  1.93 us (2%)
    pallas_call x1, Pallas kernels, body(): pl.pallas_call(kernel, out_shape=shapes, in_specs=[in_smem, in_smem, in_v...  82.8 us
    pallas_call x1, Pallas kernels, body(): pl.pallas_call(hand_over, out_shape=shapes, in_specs=[in_vmem] * 3, out_s...  2.21 us

profile of v3, /device:TPU:1, one launch (start us, length us, event | category | flops | bytes accessed | tf_op | source)
XLA Modules:
  0.0 87.0 jit_solution(747316765223629076)
XLA Ops:
  1.9 82.8 %conformer_conv.1 = (bf16[1,256,1536]{2,1,0:T(8,128)(2,1)}, f32[12,3072]{1,0:T(8,128)}, f32[12,32]{1,0:T(8,128)}) custom-call(s32[1]{0:T(128)S(6)} %copy.9.len_ref, s32[1,1]{1,0:T(1,128)S(6)} %copy.10.poi_ref, bf16[32,768]{1,0:T(8,128)(2,1)} %bitcast.1, bf16[1,256,1536]{2,1,0:T(8,128)(2,1)} %x_hbm.1, bf16[1,256,1536]{2,1,0:T(8,128)(2,1)} %cot_hbm.1, ...), custom_call_target="tpu_custom_call" | custom-call | tf_op jit(solution)/shard_map/conformer_conv/pallas_call | solution.py:681
  84.8 2.2 %hand_over.1 = (bf16[1,256,1536]{2,1,0:T(8,128)(2,1)}, f32[12,3072]{1,0:T(8,128)}, f32[12,32]{1,0:T(8,128)}) custom-call(bf16[1,256,1536]{2,1,0:T(8,128)(2,1)} %get-tuple-element.6.gx, f32[12,3072]{1,0:T(8,128)} %get-tuple-element.7.gin, f32[12,32]{1,0:T(8,128)} %get-tuple-element.8.gtap), custom_call_target="tpu_custom_call" | custom-call | tf_op jit(solution)/shard_map/hand_over/pallas_call | solution.py:692

commit v4 on v3

--- a/solution.py
+++ b/solution.py
@@ -84,6 +84,7 @@
     partners += [dev(c, z, yd(d), x) for d in (1, 2, 3)]
     partners += [dev(c, zd(d), y, x) for d in (1, 2, 3)]
     partners += [(e, q, f) for q in (prv, nxt) for e in (0, 1)]
+    partners += [dev(c, zd(d), yd(e), x) for d in (1, 2, 3) for e in (1, 2, 3)]
     barrier = pltpu.get_barrier_semaphore()
     for partner in partners:
         pl.semaphore_signal(barrier, inc=1, device_id=partner, device_id_type=MESH)
@@ -555,15 +556,17 @@
     for i in range(7):
         total = total + ps_r[i]
     ps_s[1] = total
-    for d in (1, 2, 3):
-        send(ps_s.at[1], ps_r.at[6 + d], ps_send.at[1], ps_recv.at[1], dev(c, z, yd(d), x))
-    await_bytes(ps_r.at[7:10], ps_recv.at[1])
-    total = ps_s[1] + ps_r[7] + ps_r[8] + ps_r[9]
-    ps_s[2] = total
-    for d in (1, 2, 3):
-        send(ps_s.at[2], ps_r.at[9 + d], ps_send.at[2], ps_recv.at[2], dev(c, zd(d), y, x))
-    await_bytes(ps_r.at[10:13], ps_recv.at[2])
-    total = ps_s[2] + ps_r[10] + ps_r[11] + ps_r[12]
+    count = 7
+    for d in range(4):
+        for e in range(4):
+            if d == 0 and e == 0:
+                continue
+            send(ps_s.at[1], ps_r.at[count], ps_send.at[1], ps_recv.at[1], dev(c, zd(d), yd(e), x))
+            count += 1
+    await_bytes(ps_r.at[7:22], ps_recv.at[1])
+    total = ps_s[1]
+    for i in range(7, 22):
+        total = total + ps_r[i]
     msq = total[0:1, 0:1] / jnp.float32(2 * D * D + D * KT)
     scale = 1.0 / jnp.maximum(jnp.float32(1.0), jnp.sqrt(msq))
     gin_vm[...] = gin_vm[...] * scale
@@ -594,8 +597,7 @@
     await_bytes(t_r1, t_send.at[0])
     await_bytes(t_r2, t_send.at[1])
     await_bytes(ps_r.at[0:7], ps_send.at[0])
-    await_bytes(ps_r.at[7:10], ps_send.at[1])
-    await_bytes(ps_r.at[10:13], ps_send.at[2])
+    await_bytes(ps_r.at[7:22], ps_send.at[1])
     store_gx.wait()
     store_gin.wait()
     store_gtap.wait()
@@ -658,8 +660,8 @@
         vmem((12, KT), F32),
         vmem((3, 8, 128), jnp.int32),
         vmem((3, 3, 8, 128), jnp.int32),
-        vmem((3, 8, 128), F32),
-        vmem((13, 8, 128), F32),
+        vmem((2, 8, 128), F32),
+        vmem((22, 8, 128), F32),
         dma((3,)),
         dma((NC,)), dma((NC,)), dma((NC, 2)),
         dma((7,)), dma((7,)),
@@ -668,7 +670,7 @@
         dma((NC, 2)), dma((NC, 2)),
         dma((3, 2)), dma((3, 2)),
         dma((2,)), dma((2,)),
-        dma((3,)), dma((3,)),
+        dma((2,)), dma((2,)),
     ]
     anywhere = pl.BlockSpec(memory_space=pl.ANY)
     in_vmem = pl.BlockSpec(memory_space=pltpu.VMEM)

time: 87.9 us -> 86.1 us (0.980)
  Pallas kernels: 85 us -> 84 us
    pallas_call x1, Pallas kernels: 82.8 us -> 81.8 us  [body(): pl.pallas_call(kernel, out_shape=shapes, in_specs=[in_smem, in_smem, in_v...]
where the time goes in v4:
time: 86.1 us; the launch traced here: 85.9 us
  Pallas kernels  84 us (98%)
  between operations  1.93 us (2%)
    pallas_call x1, Pallas kernels, body(): pl.pallas_call(kernel, out_shape=shapes, in_specs=[in_smem, in_smem, in_v...  81.8 us
    pallas_call x1, Pallas kernels, body(): pl.pallas_call(hand_over, out_shape=shapes, in_specs=[in_vmem] * 3, out_s...  2.21 us

profile of v4, /device:TPU:1, one launch (start us, length us, event | category | flops | bytes accessed | tf_op | source)
XLA Modules:
  0.0 85.9 jit_solution(4555181102781236339)
XLA Ops:
  1.9 81.8 %conformer_conv.1 = (bf16[1,256,1536]{2,1,0:T(8,128)(2,1)}, f32[12,3072]{1,0:T(8,128)}, f32[12,32]{1,0:T(8,128)}) custom-call(s32[1]{0:T(128)S(6)} %copy.9.len_ref, s32[1,1]{1,0:T(1,128)S(6)} %copy.10.poi_ref, bf16[32,768]{1,0:T(8,128)(2,1)} %bitcast.1, bf16[1,256,1536]{2,1,0:T(8,128)(2,1)} %x_hbm.1, bf16[1,256,1536]{2,1,0:T(8,128)(2,1)} %cot_hbm.1, ...), custom_call_target="tpu_custom_call" | custom-call | tf_op jit(solution)/shard_map/conformer_conv/pallas_call | solution.py:683
  83.7 2.2 %hand_over.1 = (bf16[1,256,1536]{2,1,0:T(8,128)(2,1)}, f32[12,3072]{1,0:T(8,128)}, f32[12,32]{1,0:T(8,128)}) custom-call(bf16[1,256,1536]{2,1,0:T(8,128)(2,1)} %get-tuple-element.6.gx, f32[12,3072]{1,0:T(8,128)} %get-tuple-element.7.gin, f32[12,32]{1,0:T(8,128)} %get-tuple-element.8.gtap), custom_call_target="tpu_custom_call" | custom-call | tf_op jit(solution)/shard_map/hand_over/pallas_call | solution.py:694

commit v5 on v4

--- a/solution.py
+++ b/solution.py
@@ -186,10 +186,10 @@
     na[own_rows, :] = dot(to_phase, nn[...]).astype(BF16)
     send(na.at[own_rows], na.at[own_rows], misc_send.at[4], misc_recv.at[4], sibling)
 
-    await_bytes(fb_r.at[0], fb_recv.at[0])
+    await_bytes(fb_r.at[0, 0:3], fb_recv.at[0])
     fb_s[1] = jnp.minimum(jnp.minimum(fb_s[0], fb_r[0, 0]), jnp.minimum(fb_r[0, 1], fb_r[0, 2]))
-    for d in (1, 2, 3):
-        send(fb_s.at[1], fb_r.at[1, d - 1], fb_send.at[1], fb_recv.at[1], dev(c, z, yd(d), x))
+    for i in range(1, 16):
+        send(fb_s.at[1], fb_r.at[1, i - 1], fb_send.at[1], fb_recv.at[1], dev(c, zd(i // 4), yd(i % 4), x))
 
     for i in range(D // 128):
         cols = pl.ds(i * 128, 128)
@@ -199,11 +199,6 @@
     for side in (0, 1):
         halo[c, side] = normalised(edges[side])[0]
     send(halo.at[c], halo.at[c], misc_send.at[5], misc_recv.at[5], sibling)
-
-    await_bytes(fb_r.at[1], fb_recv.at[1])
-    fb_s[2] = jnp.minimum(jnp.minimum(fb_s[1], fb_r[1, 0]), jnp.minimum(fb_r[1, 1], fb_r[1, 2]))
-    for d in (1, 2, 3):
-        send(fb_s.at[2], fb_r.at[2, d - 1], fb_send.at[2], fb_recv.at[2], dev(c, zd(d), y, x))
 
     await_bytes(tap_in, misc_recv.at[2])
     mine = jnp.where(f == c, jnp.float32(1.0), jnp.float32(0.0))
@@ -386,10 +381,10 @@
 
         @pl.when(j == 0)
         def _():
-            await_bytes(fb_r.at[2], fb_recv.at[2])
-            votes = jnp.minimum(
-                jnp.minimum(fb_s[2], fb_r[2, 0]), jnp.minimum(fb_r[2, 1], fb_r[2, 2])
-            )
+            await_bytes(fb_r.at[1], fb_recv.at[1])
+            votes = fb_s[1]
+            for i in range(15):
+                votes = jnp.minimum(votes, fb_r[1, i])
             masks(keep, votes, first_half)
 
         lax.fori_loop(0, 8, forward, 0, unroll=4)
@@ -590,8 +585,8 @@
     await_bytes(na.at[own_rows], misc_send.at[4])
     await_bytes(halo.at[c], misc_send.at[5])
     await_bytes(dns, misc_send.at[6])
-    for i in range(3):
-        await_bytes(fb_r.at[i], fb_send.at[i])
+    await_bytes(fb_r.at[0, 0:3], fb_send.at[0])
+    await_bytes(fb_r.at[1], fb_send.at[1])
     for q, width in ((0, 512), (1, 512), (2, 640)):
         stage3_await(q, width, r3_send)
     await_bytes(t_r1, t_send.at[0])
@@ -658,14 +653,14 @@
         vmem((ROWS, D), BF16),
         vmem((12, 2 * D), F32),
         vmem((12, KT), F32),
-        vmem((3, 8, 128), jnp.int32),
-        vmem((3, 3, 8, 128), jnp.int32),
+        vmem((2, 8, 128), jnp.int32),
+        vmem((2, 15, 8, 128), jnp.int32),
         vmem((2, 8, 128), F32),
         vmem((22, 8, 128), F32),
         dma((3,)),
         dma((NC,)), dma((NC,)), dma((NC, 2)),
         dma((7,)), dma((7,)),
-        dma((3,)), dma((3,)),
+        dma((2,)), dma((2,)),
         dma((NC, 2)), dma((NC, 2)),
         dma((NC, 2)), dma((NC, 2)),
         dma((3, 2)), dma((3, 2)),

time: 86.1 us -> 86.1 us (level)
  no operation moved by 1% of the time
where the time goes in v5:
time: 86.1 us; the launch traced here: 85.9 us
  Pallas kernels  83.9 us (97%)
  between operations  1.93 us (2%)
    pallas_call x1, Pallas kernels, body(): pl.pallas_call(kernel, out_shape=shapes, in_specs=[in_smem, in_smem, in_v...  81.7 us
    pallas_call x1, Pallas kernels, body(): pl.pallas_call(hand_over, out_shape=shapes, in_specs=[in_vmem] * 3, out_s...  2.21 us

profile of v5, /device:TPU:1, one launch (start us, length us, event | category | flops | bytes accessed | tf_op | source)
XLA Modules:
  0.0 85.9 jit_solution(17044175987862226392)
XLA Ops:
  1.9 81.7 %conformer_conv.1 = (bf16[1,256,1536]{2,1,0:T(8,128)(2,1)}, f32[12,3072]{1,0:T(8,128)}, f32[12,32]{1,0:T(8,128)}) custom-call(s32[1]{0:T(128)S(6)} %copy.9.len_ref, s32[1,1]{1,0:T(1,128)S(6)} %copy.10.poi_ref, bf16[32,768]{1,0:T(8,128)(2,1)} %bitcast.1, bf16[1,256,1536]{2,1,0:T(8,128)(2,1)} %x_hbm.1, bf16[1,256,1536]{2,1,0:T(8,128)(2,1)} %cot_hbm.1, ...), custom_call_target="tpu_custom_call" | custom-call | tf_op jit(solution)/shard_map/conformer_conv/pallas_call | solution.py:678
  83.7 2.2 %hand_over.1 = (bf16[1,256,1536]{2,1,0:T(8,128)(2,1)}, f32[12,3072]{1,0:T(8,128)}, f32[12,32]{1,0:T(8,128)}) custom-call(bf16[1,256,1536]{2,1,0:T(8,128)(2,1)} %get-tuple-element.6.gx, f32[12,3072]{1,0:T(8,128)} %get-tuple-element.7.gin, f32[12,32]{1,0:T(8,128)} %get-tuple-element.8.gtap), custom_call_target="tpu_custom_call" | custom-call | tf_op jit(solution)/shard_map/hand_over/pallas_call | solution.py:689
